TPU v7x, 128 devices: a whole 4x4x4 slice. The times are simulated.
128 devices in a mesh: seq: 8 (over z, core), dp: 16 (over x, y).
Axes of the slice: x: 4, y: 4, z: 4, core: 2. Of those that a mesh axis runs over, the one named last changes fastest.
Arguments:
- hidden_rows: bfloat16 [16, 1024, 5120], P('dp', 'seq'), may hold values from -6 to 6
- segment_ids: int32 [16, 1024], P('dp'), may hold values from 0 to 7, never falling along the last dimension, each value on 1 to 512 neighbouring positions
- block_home: int32 [16, 64], P('dp'), may hold values from 0 to 63, as said below
- input_gain: float32 [5120], replicated, may hold values from 0.5 to 1.5
- w_query: bfloat16 [5120, 8192], P('dp', 'seq'), may hold values from -0.078125 to 0.078125
- key_weight: bfloat16 [5120, 1024], P('dp', 'seq'), may hold values from -0.078125 to 0.078125
- value_weight: bfloat16 [5120, 1024], P('dp', 'seq'), may hold values from -0.078125 to 0.078125
- q_gain: float32 [128], replicated, may hold values from 0.5 to 1.5
- k_gain: float32 [128], replicated, may hold values from 0.5 to 1.5
Outputs:
- moved_context: bfloat16 [16, 1024, 8192], P('dp', 'seq')
Inputs may be any that keep to these rules, and one draw needn't show every extreme that they name: `block_home`: for each pack the entries are a permutation of the pack's block numbers; block b of the pack, as it lies in hidden_rows, is on device b // 8 of seq, and block position n lands on device n // 8; every device of seq receives exactly one block from each device of seq. `segment_ids`: never falling along a pack; each of the 8 documents has 1 to 512 positions.
All inputs are finite; a program needn't handle non-finite values.
Results may differ from a plain program's by a relative error of at most 0.0078.
Values may be sent and summed in bfloat16 or wider, within the bound.
A program may use at most 128 MiB of HBM per device.

v0:
```python
import math

import jax
import jax.numpy as jnp
from jax import lax
from jax.sharding import PartitionSpec as P

EPS = 1e-06
ROPE_BASE = 1000000.0


def as_sent(value):

    def short(part):
        return part.astype(jnp.bfloat16) if part.dtype == jnp.float32 else part

    return jax.tree.map(short, value)


def doc_positions(segments):
    row_index = jnp.arange(segments.shape[0], dtype=jnp.int32)
    previous = jnp.concatenate([segments[:1] - 1, segments[:-1]])
    starts = jnp.where(segments != previous, row_index, 0)
    return (row_index - lax.cummax(starts, axis=0)).astype(jnp.float32)


def rotary(value_rows, positions):
    half_dim = value_rows.shape[-1] // 2
    exponent = jnp.arange(half_dim, dtype=jnp.float32) * (2.0 / value_rows.shape[-1])
    frequency = jnp.exp(-math.log(ROPE_BASE) * exponent)
    angles = positions[:, None] * frequency[None, :]
    cosine = jnp.cos(angles)[:, None, :]
    sine_table = jnp.sin(angles)[:, None, :]
    first_half = value_rows[..., :half_dim]
    second = value_rows[..., half_dim:]
    return jnp.concatenate(
        [first_half * cosine - second * sine_table, second * cosine + first_half * sine_table],
        axis=-1,
    )


def head_norm(value_rows, head_gain):
    mean_square = jnp.mean(value_rows * value_rows, axis=-1, keepdims=True)
    return value_rows * lax.rsqrt(mean_square + EPS) * head_gain


def body(
    hidden_rows,
    segment_ids,
    block_home,
    input_gain,
    w_query,
    key_weight,
    value_weight,
    q_gain,
    k_gain,
):
    groups = lax.axis_size("seq")
    rows_wide = hidden_rows[0].astype(jnp.float32)
    scale_rows = lax.rsqrt(jnp.mean(rows_wide * rows_wide, axis=-1, keepdims=True) + EPS)
    normalized_input = (rows_wide * scale_rows * input_gain).astype(jnp.bfloat16)
    every_row = lax.all_gather(normalized_input, "seq", axis=0, tiled=True)
    total_rows = every_row.shape[0]
    head_dim = q_gain.shape[0]
    pieces = (
        lax.all_gather(w_query, "dp", axis=0, tiled=True),
        lax.all_gather(key_weight, "dp", axis=0, tiled=True),
        lax.all_gather(value_weight, "dp", axis=0, tiled=True),
    )
    query_raw, unnormed_key, value_raw = tuple(
        (jnp.dot(every_row, piece, preferred_element_type=jnp.float32) for piece in pieces)
    )
    q_heads = query_raw.shape[1] // head_dim
    kv_heads = unnormed_key.shape[1] // head_dim
    per_group = q_heads // kv_heads
    segments = segment_ids[0]
    positions = doc_positions(segments)
    queries = rotary(
        head_norm(query_raw.reshape(total_rows, q_heads, head_dim), q_gain), positions
    ).astype(jnp.bfloat16)
    keys_all = rotary(
        head_norm(unnormed_key.reshape(total_rows, kv_heads, head_dim), k_gain), positions
    ).astype(jnp.bfloat16)
    value_rows = value_raw.astype(jnp.bfloat16).reshape(total_rows, kv_heads, head_dim)
    block_size = min(128, total_rows)
    blocks_count = total_rows // block_size
    row_index = jnp.arange(total_rows, dtype=jnp.int32)
    score_scale = 1.0 / math.sqrt(head_dim)
    grouped = queries.reshape(blocks_count, block_size, kv_heads, per_group, head_dim)

    def attend_block(inputs):
        query_block, block_start = inputs
        query_index = block_start + jnp.arange(block_size, dtype=jnp.int32)
        query_segs = lax.dynamic_slice_in_dim(segments, block_start, block_size)
        allowed = (query_segs[:, None] == segments[None, :]) & (
            row_index[None, :] <= query_index[:, None]
        )
        allowed = jnp.broadcast_to(
            allowed[:, None, :], (block_size, per_group, total_rows)
        ).reshape(block_size * per_group, total_rows)
        flat_query = query_block[:, 0].reshape(block_size * per_group, head_dim)
        scores = (
            jnp.einsum("qd,kd->qk", flat_query, keys_all[:, 0], preferred_element_type=jnp.float32)
            * score_scale
        )
        weights = jnp.where(allowed, jnp.exp(scores), 0.0)
        totals = jnp.sum(weights, axis=-1, keepdims=True)
        mixed = (
            jnp.dot(
                weights.astype(jnp.bfloat16), value_rows[:, 0], preferred_element_type=jnp.float32
            )
            / totals
        )
        outputs = [mixed.astype(jnp.bfloat16).reshape(block_size, per_group, head_dim)]
        return jnp.stack(outputs, axis=1)

    block_starts = jnp.arange(blocks_count, dtype=jnp.int32) * block_size
    context = lax.map(attend_block, (grouped, block_starts)).reshape(total_rows, q_heads * head_dim)
    new_order = block_home[0]
    block_total = new_order.shape[0]
    per_device = block_total // groups
    block_rows = total_rows // block_total
    home = lax.all_to_all(as_sent(context), "seq", split_axis=0, concat_axis=1, tiled=True).astype(
        context.dtype
    )
    columns_all = home.shape[1]
    my_index = lax.axis_index("seq")
    block_index = jnp.arange(block_total, dtype=jnp.int32)
    new_place = jnp.sum(
        jnp.where(new_order[None, :] == block_index[:, None], block_index[None, :], 0), axis=1
    )
    mine_place = lax.dynamic_slice_in_dim(new_place, my_index * per_device, per_device)
    target_device = mine_place // per_device
    device_index = jnp.arange(groups, dtype=jnp.int32)
    slot_index = jnp.arange(per_device, dtype=jnp.int32)
    slot_for = jnp.sum(
        jnp.where(target_device[None, :] == device_index[:, None], slot_index[None, :], 0), axis=1
    )
    outgoing = jnp.take(home.reshape(per_device, block_rows, columns_all), slot_for, axis=0)
    arrived = lax.all_to_all(
        as_sent(outgoing), "seq", split_axis=0, concat_axis=0, tiled=True
    ).astype(outgoing.dtype)
    mine_new = lax.dynamic_slice_in_dim(new_order, my_index * per_device, per_device)
    moved = jnp.take(arrived, mine_new // per_device, axis=0).reshape(
        per_device * block_rows, columns_all
    )
    return moved[None]


def solution(mesh):
    return jax.shard_map(
        body,
        mesh=mesh,
        in_specs=(
            P("dp", "seq", None),
            P("dp", None),
            P("dp", None),
            P(),
            P("dp", "seq"),
            P("dp", "seq"),
            P("dp", "seq"),
            P(),
            P(),
        ),
        out_specs=P("dp", "seq", None),
        check_vma=False,
    )
```

profile of v0, /device:TPU:1, one launch (start us, length us, event | category | flops | bytes accessed | tf_op | source)
XLA Modules:
  0.0 436.0 jit_solution(10450411368563715335)
XLA Ops:
  9.0 2.2 fusion.30
  15.3 39.9 %all-gather.9.cloned.1.call-done = bf16[5120,128]{1,0:T(8,128)(2,1)} async-done(((bf16[320,128]{1,0:T(8,128)(2,1)}), bf16[5120,128]{1,0:T(8,128)(2,1)}) %all-gather.9.cloned.1.call-update) | async-done | bytes 1310736 | tf_op jit(solution)/shard_map/all_gather | solution.py:67
  55.2 61.1 %all-gather.5.cloned.1.call-done = bf16[1024,5120]{1,0:T(8,128)(2,1)} async-done(((bf16[128,5120]{1,0:T(8,128)(2,1)}), bf16[1024,5120]{1,0:T(8,128)(2,1)}) %all-gather.5.cloned.1.call-update) | async-done | bytes 10485776 | tf_op jit(solution)/shard_map/all_gather | solution.py:62
  116.3 7.9 %multiply_reduce_fusion.1 = (f32[1024]{0:T(1024)S(1)}, f32[1024,128]{0,1:T(8,128)S(1)}) fusion(bf16[1024,5120]{1,0:T(8,128)(2,1)} %all-gather.5.cloned.1.call-done, bf16[5120,128]{1,0:T(8,128)(2,1)} %all-gather.9.cloned.1.call-done), kind=kOutput, calls=%fused_computation.38 | convolution fusion | flops 1342438400 | bytes 12324864 | tf_op jit(solution)/shard_map/dot_general | solution.py:71
  125.9 34.7 %all-gather.11.cloned.1.call-done = bf16[5120,128]{1,0:T(8,128)(2,1)} async-done(((bf16[320,128]{1,0:T(8,128)(2,1)}), bf16[5120,128]{1,0:T(8,128)(2,1)}) %all-gather.11.cloned.1.call-update) | async-done | bytes 1310736 | tf_op jit(solution)/shard_map/all_gather | solution.py:68
  160.6 7.9 %convolution_convert_fusion = bf16[1024,128]{1,0:T(8,128)(2,1)} fusion(bf16[1024,5120]{1,0:T(8,128)(2,1)} %all-gather.5.cloned.1.call-done, bf16[5120,128]{1,0:T(8,128)(2,1)} %all-gather.11.cloned.1.call-done), kind=kOutput, calls=%fused_computation.36 | convolution fusion | flops 1342308352 | bytes 12058624 | tf_op jit(solution)/shard_map/dot_general | solution.py:71
  168.5 74.7 %all-gather.7.cloned.1.call-done = bf16[5120,1024]{1,0:T(8,128)(2,1)} async-done(((bf16[320,1024]{1,0:T(8,128)(2,1)}), bf16[5120,1024]{1,0:T(8,128)(2,1)}) %all-gather.7.cloned.1.call-update) | async-done | bytes 10485776 | tf_op jit(solution)/shard_map/all_gather | solution.py:66
  243.2 18.1 %multiply_reduce_fusion = (f32[1024,8]{0,1:T(8,128)S(1)}, f32[1024,1024]{0,1:T(8,128)}) fusion(bf16[1024,5120]{1,0:T(8,128)(2,1)} %all-gather.5.cloned.1.call-done, bf16[5120,1024]{1,0:T(8,128)(2,1)} %all-gather.7.cloned.1.call-done), kind=kOutput, calls=%fused_computation.25 | convolution fusion | flops 10739507200 | bytes 25198592 | tf_op jit(solution)/shard_map/dot_general | solution.py:71
  261.4 2.9 multiply_multiply_fusion
  266.0 2.6 copy.24
  268.6 2.5 copy.25
  271.1 4.1 pad_maximum_fusion
  275.3 72.1 %while.11 = (s32[]{:T(128)}, bf16[8,128,1,8,128]{4,3,1,2,0:T(8,128)(2,1)}, s32[8]{0:T(128)S(1)}, s32[1024]{0:T(1024)S(1)}, s32[1,1024]{1,0:T(1,128)S(1)}, /*inde...) while((s32[]{:T(128)}, ...), condition=%wide.region_7.8_spmd.clone, body=%wide.region_5.7_spmd.clone.sunk | while | flops 543816832 | bytes 14958243 | solution.py:118
  307.4 2.1 fusion.56
  334.4 2.1 fusion.56
  347.3 4.1 all_to_all.15
  351.5 5.2 %all-to-all-start = ((bf16[8,128,1024]{2,1,0:T(8,128)(2,1)}), bf16[8,128,1024]{2,1,0:T(8,128)(2,1)S(1)}, u32[]{:S(2)}, u32[]{:S(2)}) async-start(bf16[8,128,1024]{2,1,0:T(8,128)(2,1)} %all_to_all.15), calls=%async_computation | async-start | bytes 4194304 | tf_op jit(solution)/shard_map/all_to_all | solution.py:123
  357.1 26.0 %all-to-all-done = bf16[8,128,1024]{2,1,0:T(8,128)(2,1)S(1)} async-done(((bf16[8,128,1024]{2,1,0:T(8,128)(2,1)}), bf16[8,128,1024]{2,1,0:T(8,128)(2,1)S(1)}, u32[]{:S(2)}, u32[]{:S(2)}) %all-to-all-start) | async-done | bytes 2097184 | tf_op jit(solution)/shard_map/all_to_all | solution.py:123
  383.1 2.5 copy.27
  385.5 4.2 reshape.312
  389.7 2.3 gather_fusion
  393.6 4.4 %all-to-all-start.1 = ((bf16[8,16,8192]{2,1,0:T(8,128)(2,1)}), bf16[8,16,8192]{2,1,0:T(8,128)(2,1)S(1)}, u32[]{:S(2)}, u32[]{:S(2)}) async-start(bf16[8,16,8192]{2,1,0:T(8,128)(2,1)} %broadcast_select_fusion.1), calls=%async_computation.1 | async-start | bytes 4194304 | tf_op jit(solution)/shard_map/all_to_all | solution.py:140
  398.0 26.3 %all-to-all-done.1 = bf16[8,16,8192]{2,1,0:T(8,128)(2,1)S(1)} async-done(((bf16[8,16,8192]{2,1,0:T(8,128)(2,1)}), bf16[8,16,8192]{2,1,0:T(8,128)(2,1)S(1)}, u32[]{:S(2)}, u32[]{:S(2)}) %all-to-all-start.1) | async-done | bytes 2097184 | tf_op jit(solution)/shard_map/all_to_all | solution.py:140
  426.3 3.2 broadcast_select_fusion
  (112 shorter events, 65.8 us)
Async XLA Ops:
  6.5 2.4 copy-start
  6.5 48.6 %all-gather.9.cloned.1.call-start = ((), (), s32[]{:S(2)}) async-start(), calls=%async_computation.4 | async-start | bytes 1392640 | tf_op jit(solution)/shard_map/all_gather | solution.py:67
  7.3 109.0 %all-gather.5.cloned.1.call-start = ((), (), s32[]{:S(2)}) async-start(), calls=%async_computation.2 | async-start | bytes 11796480 | tf_op jit(solution)/shard_map/all_gather | solution.py:62
  9.0 3.6 copy-start.1
  11.2 149.4 %all-gather.11.cloned.1.call-start = ((), (), s32[]{:S(2)}) async-start(), calls=%async_computation.5 | async-start | bytes 1392640 | tf_op jit(solution)/shard_map/all_gather | solution.py:68
  11.9 231.2 %all-gather.7.cloned.1.call-start = ((), (), s32[]{:S(2)}) async-start(), calls=%async_computation.3 | async-start | bytes 11141120 | tf_op jit(solution)/shard_map/all_gather | solution.py:66
  15.2 109.0 %copy-start.2 = (f32[128]{0:T(128)S(1)}, f32[128]{0:T(128)}, u32[]{:S(2)}) copy-start(f32[128]{0:T(128)} %param.21) | copy-start | bytes 1540
  168.5 92.8 %copy-start.3 = (f32[128]{0:T(128)S(1)}, f32[128]{0:T(128)}, u32[]{:S(2)}) copy-start(f32[128]{0:T(128)} %param.20) | copy-start | bytes 1540
  271.1 4.1 copy-start.5
  351.5 5.2 %copy-start.4 = (s32[1,64]{1,0:T(1,128)S(1)}, s32[1,64]{1,0:T(1,128)}, u32[]{:S(2)}) copy-start(s32[1,64]{1,0:T(1,128)} %param.15) | copy-start | bytes 772
  351.5 31.6 %all-to-all-start = ((bf16[8,128,1024]{2,1,0:T(8,128)(2,1)}), bf16[8,128,1024]{2,1,0:T(8,128)(2,1)S(1)}, u32[]{:S(2)}, u32[]{:S(2)}) async-start(bf16[8,128,1024]{2,1,0:T(8,128)(2,1)} %all_to_all.15), calls=%async_computation | async-start | bytes 4194304 | tf_op jit(solution)/shard_map/all_to_all | solution.py:123
  393.6 30.7 %all-to-all-start.1 = ((bf16[8,16,8192]{2,1,0:T(8,128)(2,1)}), bf16[8,16,8192]{2,1,0:T(8,128)(2,1)S(1)}, u32[]{:S(2)}, u32[]{:S(2)}) async-start(bf16[8,16,8192]{2,1,0:T(8,128)(2,1)} %broadcast_select_fusion.1), calls=%async_computation.1 | async-start | bytes 4194304 | tf_op jit(solution)/shard_map/all_to_all | solution.py:140
Sparse Core Ops, SparseCore 0:
  9.5 45.5 all-gather.8
  56.9 59.4 all-gather.4
  118.5 42.0 all-gather.10
  162.7 80.4 all-gather.6
where the time goes:
time: 437 us; the launch traced here: 436 us
  waiting for transfers between devices  265 us (61%)
  matrix products  65.4 us (15%)
  local copies, waits for them, and re-layouts  39.9 us (9%)
  other arithmetic  27.3 us (6%)
  loops' own time  15.2 us (3%)
  between operations  13.9 us (3%)
  starting transfers between devices  9.74 us (2%)
    all_gather x1, waiting for transfers between devices, body(): lax.all_gather(w_query, 'dp', axis=0, tiled=True)  74.7 us
    all_gather x1, waiting for transfers between devices, body(): every_row = lax.all_gather(normalized_input, 'seq', axis=0, tiled=True)  61.1 us
    all_gather x1, waiting for transfers between devices, body(): lax.all_gather(key_weight, 'dp', axis=0, tiled=True)  39.9 us
    all_gather x1, waiting for transfers between devices, body(): lax.all_gather(value_weight, 'dp', axis=0, tiled=True)  34.7 us
    dot_general x3, matrix products, body(): jnp.dot(every_row, piece, preferred_element_type=jnp.float32)  33.9 us
    all_to_all x1, waiting for transfers between devices, body(): lax.all_to_all(as_sent(outgoing), 'seq', split_axis=0, concat_axis=0, til...  26.3 us
    all_to_all x1, waiting for transfers between devices, body(): lax.all_to_all(as_sent(context), 'seq', split_axis=0, concat_axis=1, tile...  26 us
    dot_general x8, matrix products, attend_block(): jnp.einsum('qd,kd->qk', flat_query, keys_all[:, 0], preferred_element_typ...  16.8 us
  transfers between devices with their start and end apart: 6, of which 6 were waited for; matrix products, arithmetic and copies ran while one was open for 5% of the time, Pallas kernels for 0%

commit v1 on v0

v1 whole, which is shorter than its diff:
```python
import math

import jax
import jax.numpy as jnp
from jax import lax
from jax.experimental import pallas as pl
from jax.experimental.pallas import tpu as pltpu
from jax.sharding import PartitionSpec as P

EPS = 1e-06
ROPE_BASE = 1000000.0
MESH = pl.DeviceIdType.MESH

SIDE = 4
SEQ = 8
ROWS = 1024
OWN = ROWS // SEQ
PIECE = OWN // 2
WIDTH = 5120
SHARD = WIDTH // (SIDE * SIDE)
HALF = SHARD // 2
HEAD = 128
WIDE = 2 * HEAD
CHUNKS = 5
HEADS_OUT = 1024
BLK = 16
BLOCKS = ROWS // BLK
QROWS = 256
BAND = 768
MASKED = -1e30
SCALE = math.log2(math.e) / math.sqrt(HEAD)


def place():
    s, d = lax.axis_index("seq"), lax.axis_index("dp")
    return s, d, d // SIDE, d % SIDE


def remote(src, dst, send, recv, seq, dp):
    return pltpu.make_async_remote_copy(
        src_ref=src,
        dst_ref=dst,
        send_sem=send,
        recv_sem=recv,
        device_id={"seq": seq, "dp": dp},
        device_id_type=MESH,
    )


def along(ring, step):
    _, _, x, y = place()
    if ring == 0:
        pos = (x + step + SIDE) % SIDE
        return pos * SIDE + y, pos
    pos = (y + step + SIDE) % SIDE
    return x * SIDE + pos, pos


FIRST = ((0, None, 1), (0, None, -1), (-1, 0, 1), (1, 1, -1))
SECOND = ((0, 0, 1), (0, 1, 1), (-1, 0, 1), (0, 1, -1), (0, 0, -1), (1, 1, -1))


def first_copy(b, j, half, kind, receiving=False):
    s, _, x, y = place()
    whose, part, way = FIRST[kind]
    target, _ = along(half, way)
    _, pos = along(half, whose - way if receiving else whose)
    rows = pl.ds(0, HALF) if part is None else pl.ds(part * (HALF // 2), HALF // 2)
    view = b.weights.at[j, pos, y, 0, rows] if half == 0 else b.weights.at[j, x, pos, 1, rows]
    return remote(view, view, b.first_send.at[j, half, kind], b.first_recv.at[j, half, kind], s, target)


def second_copy(b, j, half, kind, receiving=False):
    s, _, _, _ = place()
    whose, part, way = SECOND[kind]
    ring = 1 - half
    target, _ = along(ring, way)
    _, pos = along(ring, whose - way if receiving else whose)
    line = pl.ds(2 * part, 2)
    view = b.weights.at[j, line, pos, 0] if half == 0 else b.weights.at[j, pos, line, 1]
    return remote(view, view, b.second_send.at[j, half, kind], b.second_recv.at[j, half, kind], s, target)


def shard_rows(b, owner, part):
    if part is None:
        return b.rows.at[pl.ds(pl.multiple_of(owner * OWN, OWN), OWN)]
    return b.rows.at[pl.ds(pl.multiple_of(owner * OWN + part * PIECE, PIECE), PIECE)]


def row_copy(b, kind, receiving=False):
    s, d, _, _ = place()
    whose, part, way = SECOND[kind]
    target = (s + 2 * way + SEQ) % SEQ
    owner = (s + 2 * (whose - way if receiving else whose) + 2 * SEQ) % SEQ
    view = shard_rows(b, owner, part)
    return remote(view, view, b.row_send.at[kind], b.row_recv.at[kind], target, d)


def twin_copy(b, kind, receiving=False):
    s, d, _, _ = place()
    twin = s + 1 - 2 * (s % 2)
    base = twin if receiving else s
    if kind == 6:
        view = shard_rows(b, base, None)
    else:
        whose, part, way = SECOND[kind]
        view = shard_rows(b, (base + 2 * (whose - way) + 2 * SEQ) % SEQ, part)
    return remote(view, view, b.twin_send.at[kind], b.twin_recv.at[kind], twin, d)


def out_columns(b, owner, j):
    return b.out.at[0, :, pl.ds(pl.multiple_of(owner * HEADS_OUT + j * WIDE, WIDE), WIDE)]


def context_copy(b, j, step, receiving=False):
    s, d, _, _ = place()
    target = (s + step) % SEQ
    owner = (s - step + SEQ) % SEQ if receiving else s
    return remote(b.send.at[j, target], out_columns(b, owner, j), b.context_send.at[j, step - 1], b.context_recv.at[j, step - 1], target, d)


def own_context_copy(b, j):
    s, _, _, _ = place()
    return pltpu.make_async_copy(b.send.at[j, s], out_columns(b, s, j), b.local.at[j])


def own_weight_copies(b, j):
    _, _, x, y = place()
    mine = b.weights.at[j, x, y]
    if j == 0:
        return (
            pltpu.make_async_copy(b.key_weight, mine.at[:, :, pl.ds(0, HEAD)], b.own.at[0]),
            pltpu.make_async_copy(b.value_weight, mine.at[:, :, pl.ds(HEAD, HEAD)], b.own.at[1]),
        )
    return (pltpu.make_async_copy(b.w_query.at[:, :, pl.ds((j - 1) * WIDE, WIDE)], mine, b.own.at[j + 1]),)


def normalize(b):
    s, _, _, _ = place()

    @pl.loop(0, OWN // BLK)
    def _(i):
        at = pl.multiple_of(i * BLK, BLK)
        wide = b.hidden_here[pl.ds(at, BLK), :].astype(jnp.float32)
        scale = lax.rsqrt(jnp.mean(wide * wide, axis=-1, keepdims=True) + EPS)
        to = pl.multiple_of(s * OWN + at, BLK)
        b.rows[pl.ds(to, BLK), :] = (wide * scale * b.input_gain[...]).astype(jnp.bfloat16)


def tables(b):
    every = b.segments[...].astype(jnp.float32)
    counts = [jnp.sum(jnp.where(every == v, 1.0, 0.0), axis=1, keepdims=True) for v in range(SEQ - 1)]
    lane = lax.broadcasted_iota(jnp.int32, (1, HEAD), 1)
    exponent = (lane % (HEAD // 2)).astype(jnp.float32) * (2.0 / HEAD)
    frequency = jnp.exp(-math.log(ROPE_BASE) * exponent)
    sign = jnp.where(lane < HEAD // 2, -1.0, 1.0)
    down = lax.broadcasted_iota(jnp.int32, (HEAD, HEAD), 0)
    across = lax.broadcasted_iota(jnp.int32, (HEAD, HEAD), 1)
    step = lax.broadcasted_iota(jnp.int32, (HEAD, 1), 0)
    reach = lax.broadcasted_iota(jnp.int32, (HEAD, BAND), 1)

    @pl.loop(0, ROWS // HEAD)
    def _(i):
        at = pl.multiple_of(i * HEAD, HEAD)
        here = b.segments[:, pl.ds(at, HEAD)].astype(jnp.float32)
        column = jnp.sum(jnp.where(down == across, here, 0.0), axis=1, keepdims=True)
        start = jnp.zeros_like(column)
        for v, count in enumerate(counts):
            start = start + jnp.where(column > v, count, 0.0)
        place_of = (step + at).astype(jnp.float32)
        angle = (place_of - start) * frequency
        b.cosine[pl.ds(at, HEAD), :] = jnp.cos(angle)
        b.sine[pl.ds(at, HEAD), :] = jnp.sin(angle) * sign
        key = (reach + ((i // 2) * QROWS + QROWS - BAND)).astype(jnp.float32)
        allowed = (key >= start) & (key <= place_of)
        b.bias[pl.ds(at, HEAD), :] = jnp.where(allowed, 0.0, MASKED)


def turned(b, raw, gain, at):
    scale = lax.rsqrt(jnp.mean(raw * raw, axis=-1, keepdims=True) + EPS)
    normed = raw * scale * gain
    turn = normed * b.cosine[at, :] + pltpu.roll(normed, HEAD // 2, 1) * b.sine[at, :]
    return turn.astype(jnp.bfloat16)


def project(b, j, keys):
    piece = b.weights.at[j].reshape(WIDTH, WIDE)

    @pl.loop(0, ROWS // QROWS)
    def _(i):
        at = pl.ds(pl.multiple_of(i * QROWS, QROWS), QROWS)
        raw = jnp.dot(b.rows[at, :], piece[...], preferred_element_type=jnp.float32)
        if keys:
            b.keys[at, :] = turned(b, raw[:, :HEAD], b.k_gain[...], at)
            b.values[at, :] = raw[:, HEAD:].astype(jnp.bfloat16)
        else:
            for h in range(2):
                b.queries[h, at, :] = turned(b, raw[:, h * HEAD : (h + 1) * HEAD], b.q_gain[...], at)


def attend(b):
    @pl.loop(0, 2)
    def _(h):
        columns = pl.ds(pl.multiple_of(h * HEAD, HEAD), HEAD)
        for i in range(ROWS // QROWS):
            reach = min((i + 1) * QROWS, BAND)
            keys = pl.ds((i + 1) * QROWS - reach, reach)
            at = pl.ds(i * QROWS, QROWS)
            scores = lax.dot_general(
                b.queries[h, at, :], b.keys[keys, :], (((1,), (1,)), ((), ())), preferred_element_type=jnp.float32
            )
            weights = jnp.exp2(scores * SCALE + b.bias[at, BAND - reach :])
            total = jnp.sum(weights, axis=1, keepdims=True)
            mixed = jnp.dot(weights.astype(jnp.bfloat16), b.values[keys, :], preferred_element_type=jnp.float32)
            context = (mixed / total).astype(jnp.bfloat16)
            b.context[pl.ds(i * (QROWS // BLK), QROWS // BLK), :, columns] = context.reshape(QROWS // BLK, BLK, HEAD)


def reorder(b, j):
    per = BLOCKS // SEQ

    @pl.loop(0, SEQ)
    def _(t):
        for r in range(per):
            b.send[j, t, pl.ds(r * BLK, BLK), :] = b.context[b.home[0, t * per + r]]


def barrier():
    s, d, _, _ = place()
    ready = pltpu.get_barrier_semaphore()
    for ring in range(2):
        for step in (1, -1):
            target, _ = along(ring, step)
            pl.semaphore_signal(ready, inc=1, device_id={"seq": s, "dp": target}, device_id_type=MESH)
    for step in range(1, SEQ):
        pl.semaphore_signal(ready, inc=1, device_id={"seq": (s + step) % SEQ, "dp": d}, device_id_type=MESH)
    pl.semaphore_wait(ready, 4 + SEQ - 1)


def begin_second(b, j):
    for kind in (0, 3, 1, 4):
        for half in range(2):
            second_copy(b, j, half, kind).start()


def pass_second(b, j):
    for kind in (0, 3):
        for half in range(2):
            second_copy(b, j, half, kind, True).wait_recv()
            second_copy(b, j, half, kind + 2).start()


def finish_second(b, j):
    for kind in (1, 4, 2, 5):
        for half in range(2):
            second_copy(b, j, half, kind, True).wait_recv()


class Buffers:
    def __init__(self, names, refs):
        self.__dict__.update(zip(names, refs, strict=True))


SCRATCH = {
    "rows": pltpu.VMEM((ROWS, WIDTH), jnp.bfloat16),
    "weights": pltpu.VMEM((CHUNKS, SIDE, SIDE, 2, HALF, WIDE), jnp.bfloat16),
    "hidden_here": pltpu.VMEM((OWN, WIDTH), jnp.bfloat16),
    "cosine": pltpu.VMEM((ROWS, HEAD), jnp.float32),
    "sine": pltpu.VMEM((ROWS, HEAD), jnp.float32),
    "bias": pltpu.VMEM((ROWS, BAND), jnp.float32),
    "keys": pltpu.VMEM((ROWS, HEAD), jnp.bfloat16),
    "values": pltpu.VMEM((ROWS, HEAD), jnp.bfloat16),
    "queries": pltpu.VMEM((2, ROWS, HEAD), jnp.bfloat16),
    "context": pltpu.VMEM((BLOCKS, BLK, WIDE), jnp.bfloat16),
    "send": pltpu.VMEM((CHUNKS - 1, SEQ, OWN, WIDE), jnp.bfloat16),
    "own": pltpu.SemaphoreType.DMA((CHUNKS + 2,)),
    "local": pltpu.SemaphoreType.DMA((CHUNKS - 1,)),
    "first_send": pltpu.SemaphoreType.DMA((CHUNKS, 2, 4)),
    "first_recv": pltpu.SemaphoreType.DMA((CHUNKS, 2, 4)),
    "second_send": pltpu.SemaphoreType.DMA((CHUNKS, 2, 6)),
    "second_recv": pltpu.SemaphoreType.DMA((CHUNKS, 2, 6)),
    "row_send": pltpu.SemaphoreType.DMA((6,)),
    "row_recv": pltpu.SemaphoreType.DMA((6,)),
    "twin_send": pltpu.SemaphoreType.DMA((7,)),
    "twin_recv": pltpu.SemaphoreType.DMA((7,)),
    "context_send": pltpu.SemaphoreType.DMA((CHUNKS - 1, SEQ - 1)),
    "context_recv": pltpu.SemaphoreType.DMA((CHUNKS - 1, SEQ - 1)),
}
OPERANDS = ("hidden", "segments", "home", "input_gain", "q_gain", "k_gain", "w_query", "key_weight", "value_weight", "out")


def kernel(*refs):
    b = Buffers(OPERANDS + tuple(SCRATCH), refs)
    hidden_copy = pltpu.make_async_copy(b.hidden.at[0], b.hidden_here, b.own.at[CHUNKS + 1])
    hidden_copy.start()
    for j in range(CHUNKS):
        for copy in own_weight_copies(b, j):
            copy.start()
    barrier()

    for j in range(CHUNKS):
        for copy in own_weight_copies(b, j):
            copy.wait()
        for kind in (0, 1):
            for half in range(2):
                first_copy(b, j, half, kind).start()

    hidden_copy.wait()
    normalize(b)
    for kind in (0, 3, 1, 4):
        row_copy(b, kind).start()
    twin_copy(b, 6).start()

    @pl.loop(0, CHUNKS)
    def _(j):
        for kind in (0, 1):
            for half in range(2):
                first_copy(b, j, half, kind, True).wait_recv()
                first_copy(b, j, half, kind + 2).start()

    def finish_first(j):
        for kind in (2, 3):
            for half in range(2):
                first_copy(b, j, half, kind, True).wait_recv()

    finish_first(0)
    begin_second(b, 0)
    tables(b)
    for kind in (0, 3):
        row_copy(b, kind, True).wait_recv()
        row_copy(b, kind + 2).start()
        twin_copy(b, kind).start()
    for j in range(3):
        pass_second(b, j)
        finish_first(j + 1)
        begin_second(b, j + 1)
    for kind in (1, 4, 2, 5):
        row_copy(b, kind, True).wait_recv()
        twin_copy(b, kind).start()
    for kind in range(7):
        twin_copy(b, kind, True).wait_recv()

    finish_second(b, 0)
    project(b, 0, True)

    @pl.loop(1, CHUNKS)
    def _(j):
        finish_second(b, j)
        project(b, j, False)

        @pl.when(j == 1)
        def _():
            pass_second(b, 3)
            finish_first(4)
            begin_second(b, 4)

        @pl.when(j == 2)
        def _():
            pass_second(b, 4)

        attend(b)
        reorder(b, j - 1)
        for step in range(1, SEQ):
            context_copy(b, j - 1, step).start()
        own_context_copy(b, j - 1).start()

    @pl.loop(0, CHUNKS)
    def _(j):
        for half in range(2):
            for kind in range(4):
                first_copy(b, j, half, kind).wait_send()
            for kind in range(6):
                second_copy(b, j, half, kind).wait_send()

    for kind in range(6):
        row_copy(b, kind).wait_send()
    for kind in range(7):
        twin_copy(b, kind).wait_send()

    @pl.loop(0, CHUNKS - 1)
    def _(j):
        own_context_copy(b, j).wait()
        for step in range(1, SEQ):
            context_copy(b, j, step).wait_send()
            context_copy(b, j, step, True).wait_recv()


def body(hidden_rows, segment_ids, block_home, input_gain, w_query, key_weight, value_weight, q_gain, k_gain):
    anywhere = pl.BlockSpec(memory_space=pl.ANY)
    vector = pl.BlockSpec(memory_space=pltpu.VMEM)
    scalar = pl.BlockSpec(memory_space=pltpu.SMEM)
    return pl.pallas_call(
        kernel,
        out_shape=jax.ShapeDtypeStruct((1, OWN, SEQ * HEADS_OUT), jnp.bfloat16),
        in_specs=[anywhere, vector, scalar, vector, vector, vector, anywhere, anywhere, anywhere],
        out_specs=anywhere,
        scratch_shapes=list(SCRATCH.values()),
        compiler_params=pltpu.CompilerParams(
            collective_id=0, has_side_effects=True, vmem_limit_bytes=56 * 1024 * 1024
        ),
        name="packed_attention",
    )(
        hidden_rows,
        segment_ids,
        block_home,
        input_gain.reshape(1, WIDTH),
        q_gain.reshape(1, HEAD),
        k_gain.reshape(1, HEAD),
        w_query.reshape(2, HALF, HEADS_OUT),
        key_weight.reshape(2, HALF, HEAD),
        value_weight.reshape(2, HALF, HEAD),
    )


def solution(mesh):
    return jax.shard_map(
        body,
        mesh=mesh,
        in_specs=(
            P("dp", "seq", None),
            P("dp", None),
            P("dp", None),
            P(),
            P("dp", "seq"),
            P("dp", "seq"),
            P("dp", "seq"),
            P(),
            P(),
        ),
        out_specs=P("dp", "seq", None),
        check_vma=False,
    )
```

time: 437 us -> 103 us (0.24)
  waiting for transfers between devices: 265 us -> 0 us
  Pallas kernels: 0 us -> 99.4 us
  matrix products: 65.4 us -> 0 us
  local copies, waits for them, and re-layouts: 39.9 us -> 3.1 us
  other arithmetic: 27.3 us -> 0 us
  loops' own time: 15.2 us -> 0 us
  between operations: 13.9 us -> 0.01 us
  starting transfers between devices: 9.74 us -> 0 us
    all_gather x4 -> x0, waiting for transfers between devices: 210 us -> none  [the longest x1 74.7 us: body(): lax.all_gather(w_query, 'dp', axis=0, tiled=True)]
    pallas_call x0 -> x1, Pallas kernels: none -> 99.4 us  [body(): pl.pallas_call(kernel, out_shape=jax.ShapeDtypeStruct((1, OWN, SEQ * HEAD...]
    dot_general x19 -> x0, matrix products: 65.4 us -> none  [the longest x3 33.9 us: body(): jnp.dot(every_row, piece, preferred_element_type=jnp.float32)]
    all_to_all x2 -> x0, waiting for transfers between devices: 52.2 us -> none  [the longest x1 26.3 us: body(): lax.all_to_all(as_sent(outgoing), 'seq', split_axis=0, concat_axis=0, til...]
    reshape x17 -> x0, local copies, waits for them, and re-layouts: 17.3 us -> none  [the longest x16 13.1 us: attend_block(): allowed = jnp.broadcast_to(allowed[:, None, :], (block_size, per_group, t...]
    another operation x1 -> x0, loops' own time: 15.2 us -> none  [body(): lax.map(attend_block, (grouped, block_starts))]
    all_to_all x2 -> x0, starting transfers between devices: 9.62 us -> none  [the longest x1 5.24 us: body(): lax.all_to_all(as_sent(context), 'seq', split_axis=0, concat_axis=1, tile...]
    all_to_all x2 -> x0, local copies, waits for them, and re-layouts: 6.61 us -> none  [body(): lax.all_to_all(as_sent(context), 'seq', split_axis=0, concat_axis=1, tile...]
  transfers between devices with their start and end apart: 6 -> 0, of which waited for: 6 -> 0; matrix products, arithmetic and copies ran while one was open for 5% -> 0% of each run, Pallas kernels for 0% -> 0%
where the time goes in v1:
time: 103 us
  Pallas kernels  99.4 us (97%)
  local copies, waits for them, and re-layouts  3.1 us (3%)
    pallas_call x1, Pallas kernels, body(): pl.pallas_call(kernel, out_shape=jax.ShapeDtypeStruct((1, OWN, SEQ * HEAD...  99.4 us
    unnamed x1, local copies, waits for them, and re-layouts  3.1 us

profile of v1, /device:TPU:1, one launch (start us, length us, event | category | flops | bytes accessed | tf_op | source)
XLA Modules:
  0.0 102.5 jit_solution(14873310358854989912)
XLA Ops:
  0.0 99.4 %packed_attention.1 = bf16[1,128,8192]{2,1,0:T(8,128)(2,1)} custom-call(bf16[1,128,5120]{2,1,0:T(8,128)(2,1)} %refs_0_.1, s32[1,1024]{1,0:T(1,128)} %refs_1_.1, s32[1,64]{1,0:T(1,128)} %refs_2_.1, f32[1,5120]{1,0:T(1,128)} %bitcast.9, f32[1,128]{1,0:T(1,128)} %bitcast.10, f32[1,128]{1,0:T(1,128)} %bitcast.11, bf16[2,160,1024]{2,1,0:T(8,128)(2,1)} %bitcast.6, ...), custom_call_target="tpu_custom_call" | custom-call | tf_op jit(solution)/shard_map/packed_attention/pallas_call | solution.py:392
  99.4 3.1 %copy.11 = bf16[1,128,8192]{2,1,0:T(8,128)(2,1)} copy(bf16[1,128,8192]{2,1,0:T(8,128)(2,1)} %packed_attention.1) | data formatting | bytes 4194304

commit v2 on v1

v2 whole, which is shorter than its diff:
```python
import math

import jax
import jax.numpy as jnp
from jax import lax
from jax.experimental import pallas as pl
from jax.experimental.pallas import tpu as pltpu
from jax.sharding import PartitionSpec as P

EPS = 1e-06
ROPE_BASE = 1000000.0
MESH = pl.DeviceIdType.MESH

SIDE = 4
SEQ = 8
ROWS = 1024
OWN = ROWS // SEQ
PIECE = OWN // 2
WIDTH = 5120
SHARD = WIDTH // (SIDE * SIDE)
HALF = SHARD // 2
LINE = SIDE * HALF
LINES = 2 * SIDE
PIECES = LINES * SIDE
HEAD = 128
HEADS = 8
NDOC = 8
WIDE_CHUNKS = 4
NARROW_CHUNKS = 2
CHUNKS = WIDE_CHUNKS + NARROW_CHUNKS
BLK = 16
BLOCKS = ROWS // BLK
QROWS = 256
BAND = 768
MASKED = -1e30
SCALE = math.log2(math.e) / math.sqrt(HEAD)


def place():
    s, d = lax.axis_index("seq"), lax.axis_index("dp")
    return s, d, d // SIDE, d % SIDE


def remote(src, dst, send, recv, seq, dp):
    return pltpu.make_async_remote_copy(
        src_ref=src,
        dst_ref=dst,
        send_sem=send,
        recv_sem=recv,
        device_id={"seq": seq, "dp": dp},
        device_id_type=MESH,
    )


def along(ring, step):
    _, _, x, y = place()
    if ring == 0:
        pos = (x + step + SIDE) % SIDE
        return pos * SIDE + y, pos
    pos = (y + step + SIDE) % SIDE
    return x * SIDE + pos, pos


def chunk(b, j):
    return b.wide.at[j] if j < WIDE_CHUNKS else b.narrow.at[j - WIDE_CHUNKS]


def arrived(b, view, sem):
    s, d, _, _ = place()
    remote(view, view, b.context_send, sem, s, d).wait_recv()


def left(b, view, sem):
    s, d, _, _ = place()
    remote(view, view, sem, b.context_recv, s, d).wait_send()


FIRST = ((0, None, 1), (0, None, -1), (-1, 0, 1), (1, 1, -1))
SECOND = ((0, 0, 1), (0, 1, 1), (-1, 0, 1), (0, 1, -1), (0, 0, -1), (1, 1, -1))


def first_send(b, j, kind):
    s, _, x, y = place()
    whose, part, way = FIRST[kind]
    rows = pl.ds(0, HALF) if part is None else pl.ds(part * (HALF // 2), HALF // 2)
    for half in range(2):
        target, _ = along(half, way)
        _, pos = along(half, whose)
        line = half * SIDE + (y if half == 0 else x)
        view = chunk(b, j).at[line * SIDE + pos, rows]
        remote(view, view, b.weight_send.at[j], b.weight_recv.at[j, 0 if kind < 2 else 1], s, target).start()


def second_send(b, j, kind):
    s, _, _, _ = place()
    whose, part, way = SECOND[kind]
    for half in range(2):
        target, _ = along(1 - half, way)
        _, pos = along(1 - half, whose)
        view = chunk(b, j).at[pl.ds((half * SIDE + pos) * SIDE + 2 * part, 2)]
        sem = {0: 2, 3: 2, 1: 3, 4: 3, 2: 4, 5: 4}[kind]
        remote(view, view, b.weight_send.at[j], b.weight_recv.at[j, sem], s, target).start()


def begin_first(b, j):
    for kind in (0, 1):
        first_send(b, j, kind)


def pass_first(b, j):
    arrived(b, chunk(b, j).at[pl.ds(0, 4)], b.weight_recv.at[j, 0])
    for kind in (2, 3):
        first_send(b, j, kind)


def begin_second(b, j, part):
    if part == 0:
        arrived(b, chunk(b, j).at[pl.ds(0, 2)], b.weight_recv.at[j, 1])
    for kind in ((0, 3), (1, 4))[part]:
        second_send(b, j, kind)


def pass_second(b, j):
    arrived(b, chunk(b, j).at[pl.ds(0, 8)], b.weight_recv.at[j, 2])
    for kind in (2, 5):
        second_send(b, j, kind)
    if j + 1 < CHUNKS:
        begin_second(b, j + 1, 1)
    if j + 2 < CHUNKS:
        begin_second(b, j + 2, 0)


def rows_of(b, owner, part):
    if part is None:
        return b.rows.at[pl.ds(pl.multiple_of(owner * OWN, OWN), OWN)]
    return b.rows.at[pl.ds(pl.multiple_of(owner * OWN + part * PIECE, PIECE), PIECE)]


def row_send(b, kind):
    s, d, _, _ = place()
    whose, part, way = SECOND[kind]
    view = rows_of(b, (s + 2 * whose + SEQ) % SEQ, part)
    target = (s + 2 * way + SEQ) % SEQ
    remote(view, view, b.row_send, b.row_recv.at[{0: 0, 3: 0, 1: 1, 4: 1, 2: 2, 5: 2}[kind]], target, d).start()


def rows_arrived(b, group):
    s, d, _, _ = place()
    arrived(b, b.rows.at[pl.ds(0, OWN)], b.row_recv.at[group])
    if group == 0:
        for kind in (2, 5):
            row_send(b, kind)
    twin = s + 1 - 2 * (s % 2)
    for kind in ((0, 3), (1, 4), (2, 5))[group]:
        whose, part, way = SECOND[kind]
        view = rows_of(b, (s + 2 * (whose - way) + SEQ) % SEQ, part)
        remote(view, view, b.twin_send, b.twin_recv.at[group], twin, d).start()


def twin_arrived(b, group):
    arrived(b, b.rows.at[pl.ds(0, OWN)], b.twin_recv.at[group])


def begin_rows(b):
    s, d, _, _ = place()
    for kind in (0, 3, 1, 4):
        row_send(b, kind)
    twin = s + 1 - 2 * (s % 2)
    view = rows_of(b, s, None)
    remote(view, view, b.twin_send, b.twin_recv.at[3], twin, d).start()


def send_context(b, head):
    s, d, _, _ = place()
    columns = pl.ds(pl.multiple_of((s * HEADS + head) * HEAD, HEAD), HEAD)
    for step in range(1, SEQ):
        target = (s + step) % SEQ
        remote(b.send.at[head, target], b.out.at[0, :, columns], b.context_send, b.context_recv, target, d).start()
    pltpu.make_async_copy(b.send.at[head, s], b.out.at[0, :, columns], b.context_own).start()


def finish_context(b):
    arrived(b, b.send.at[:, pl.ds(0, SEQ - 1)], b.context_recv)
    left(b, b.send.at[:, pl.ds(0, SEQ - 1)], b.context_send)
    pltpu.make_async_copy(b.send.at[:, 0], b.send.at[:, 0], b.context_own).wait()


def begin_own(b, j):
    _, _, x, y = place()
    for half in range(2):
        mine = chunk(b, j).at[(half * SIDE + (y if half == 0 else x)) * SIDE + (x if half == 0 else y)]
        if j == 0:
            parts = ((b.key_weight.at[half], mine.at[:, pl.ds(0, HEAD)]), (b.value_weight.at[half], mine.at[:, pl.ds(HEAD, HEAD)]))
        else:
            size = 2 * HEAD if j < WIDE_CHUNKS else HEAD
            start = (j - 1) * 2 * HEAD if j < WIDE_CHUNKS else (WIDE_CHUNKS - 1) * 2 * HEAD + (j - WIDE_CHUNKS) * HEAD
            parts = ((b.w_query.at[half, :, pl.ds(start, size)], mine),)
        for src, dst in parts:
            pltpu.make_async_copy(src, dst, b.own.at[j]).start()


def finish_own(b, j):
    view = chunk(b, j).at[pl.ds(0, 2)]
    pltpu.make_async_copy(view, view, b.own.at[j]).wait()


def normalize(b):
    s, _, _, _ = place()

    @pl.loop(0, OWN // BLK)
    def _(i):
        at = pl.multiple_of(i * BLK, BLK)
        wide = b.hidden_here[pl.ds(at, BLK), :].astype(jnp.float32)
        scale = lax.rsqrt(jnp.mean(wide * wide, axis=-1, keepdims=True) + EPS)
        normed = wide * scale * b.input_gain[...]
        parts = [None] * PIECES
        for x in range(SIDE):
            for y in range(SIDE):
                start = (x * SIDE + y) * SHARD
                parts[y * SIDE + x] = normed[:, start : start + HALF]
                parts[(SIDE + x) * SIDE + y] = normed[:, start + HALF : start + SHARD]
        to = pl.multiple_of(s * OWN + at, BLK)
        b.rows[pl.ds(to, BLK), :] = jnp.concatenate(parts, axis=1).astype(jnp.bfloat16)


def tables(b):
    every = b.segments[...].astype(jnp.float32)
    counts = [jnp.sum(jnp.where(every == v, 1.0, 0.0), axis=1, keepdims=True) for v in range(NDOC - 1)]
    lane = lax.broadcasted_iota(jnp.int32, (1, HEAD), 1)
    exponent = (lane % (HEAD // 2)).astype(jnp.float32) * (2.0 / HEAD)
    frequency = jnp.exp(-math.log(ROPE_BASE) * exponent)
    sign = jnp.where(lane < HEAD // 2, -1.0, 1.0)
    down = lax.broadcasted_iota(jnp.int32, (HEAD, HEAD), 0)
    across = lax.broadcasted_iota(jnp.int32, (HEAD, HEAD), 1)
    step = lax.broadcasted_iota(jnp.int32, (HEAD, 1), 0)
    reach = lax.broadcasted_iota(jnp.int32, (HEAD, BAND), 1)

    @pl.loop(0, ROWS // HEAD)
    def _(i):
        at = pl.multiple_of(i * HEAD, HEAD)
        here = b.segments[:, pl.ds(at, HEAD)].astype(jnp.float32)
        column = jnp.sum(jnp.where(down == across, here, 0.0), axis=1, keepdims=True)
        start = jnp.zeros_like(column)
        for v, count in enumerate(counts):
            start = start + jnp.where(column > v, count, 0.0)
        place_of = (step + at).astype(jnp.float32)
        angle = (place_of - start) * frequency
        b.cosine[pl.ds(at, HEAD), :] = jnp.cos(angle)
        b.sine[pl.ds(at, HEAD), :] = jnp.sin(angle) * sign
        key = (reach + ((i // 2) * QROWS + QROWS - BAND)).astype(jnp.float32)
        allowed = (key >= start) & (key <= place_of)
        b.bias[pl.ds(at, HEAD), :] = jnp.where(allowed, 0.0, MASKED)


def turned(b, raw, gain, at):
    scale = lax.rsqrt(jnp.mean(raw * raw, axis=-1, keepdims=True) + EPS)
    normed = raw * scale * gain
    turn = normed * b.cosine[at, :] + pltpu.roll(normed, HEAD // 2, 1) * b.sine[at, :]
    return turn.astype(jnp.bfloat16)


def chip_rows(k):
    s, _, _, _ = place()
    return pl.ds(pl.multiple_of((s // 2 + k) % SIDE * QROWS, QROWS), QROWS)


def project_keys(b, at):
    raw = jnp.dot(b.rows[at, :], b.wide.at[0].reshape(WIDTH, 2 * HEAD)[...], preferred_element_type=jnp.float32)
    b.keys[at, :] = turned(b, raw[:, :HEAD], b.k_gain[...], at)
    b.values[at, :] = raw[:, HEAD:].astype(jnp.bfloat16)


def keep_queries(b, raw, at):
    for h in range(raw.shape[1] // HEAD):
        b.queries[h, at, :] = turned(b, raw[:, h * HEAD : (h + 1) * HEAD], b.q_gain[...], at)


def project_queries(b, at):
    raw = jnp.dot(b.rows[at, :], b.wide.at[1].reshape(WIDTH, 2 * HEAD)[...], preferred_element_type=jnp.float32)
    keep_queries(b, raw, at)


def lines_product(b, piece, at, late):
    _, _, x, y = place()
    left_sides, right_sides = [], []
    for half, mine in ((0, y), (1, x)):
        for step in (2,) if late else (0, 1, 3):
            line = half * SIDE + (mine + step) % SIDE
            left_sides.append(b.rows[at, pl.ds(pl.multiple_of(line * LINE, HEAD), LINE)])
            right_sides.append(piece[pl.ds(line * SIDE, SIDE)].reshape(LINE, piece.shape[-1]))
    return jnp.dot(
        jnp.concatenate(left_sides, axis=1), jnp.concatenate(right_sides, axis=0), preferred_element_type=jnp.float32
    )


def project_early(b, piece):
    columns = pl.ds(0, piece.shape[-1])
    for i in range(ROWS // QROWS):
        at = pl.ds(i * QROWS, QROWS)
        b.partial[at, columns] = lines_product(b, piece, at, False)


def project_late(b, piece):
    columns = pl.ds(0, piece.shape[-1])
    for i in range(ROWS // QROWS):
        at = pl.ds(i * QROWS, QROWS)
        keep_queries(b, b.partial[at, columns] + lines_product(b, piece, at, True), at)


def attend(b, slot, head):
    for i in range(ROWS // QROWS):
        reach = min((i + 1) * QROWS, BAND)
        keys = pl.ds((i + 1) * QROWS - reach, reach)
        at = pl.ds(i * QROWS, QROWS)
        scores = lax.dot_general(
            b.queries[slot, at, :], b.keys[keys, :], (((1,), (1,)), ((), ())), preferred_element_type=jnp.float32
        )
        weights = jnp.exp2(scores * SCALE + b.bias[at, BAND - reach :])
        total = jnp.sum(weights, axis=1, keepdims=True)
        mixed = jnp.dot(weights.astype(jnp.bfloat16), b.values[keys, :], preferred_element_type=jnp.float32)
        context = (mixed / total).astype(jnp.bfloat16)
        b.context[pl.ds(i * (QROWS // BLK), QROWS // BLK)] = context.reshape(QROWS // BLK, BLK, HEAD)
    per = BLOCKS // SEQ
    for t in range(SEQ):
        for r in range(per):
            b.send[head, t, pl.ds(r * BLK, BLK), :] = b.context[b.home[0, t * per + r]]
    send_context(b, head)


def barrier():
    s, d, _, _ = place()
    ready = pltpu.get_barrier_semaphore()
    for ring in range(2):
        for step in (1, -1):
            target, _ = along(ring, step)
            pl.semaphore_signal(ready, inc=1, device_id={"seq": s, "dp": target}, device_id_type=MESH)
    for step in range(1, SEQ):
        pl.semaphore_signal(ready, inc=1, device_id={"seq": (s + step) % SEQ, "dp": d}, device_id_type=MESH)
    pl.semaphore_wait(ready, 4 + SEQ - 1)


class Buffers:
    def __init__(self, names, refs):
        self.__dict__.update(zip(names, refs, strict=True))


SCRATCH = {
    "rows": pltpu.VMEM((ROWS, WIDTH), jnp.bfloat16),
    "wide": pltpu.VMEM((WIDE_CHUNKS, PIECES, HALF, 2 * HEAD), jnp.bfloat16),
    "narrow": pltpu.VMEM((NARROW_CHUNKS, PIECES, HALF, HEAD), jnp.bfloat16),
    "hidden_here": pltpu.VMEM((OWN, WIDTH), jnp.bfloat16),
    "segments": pltpu.VMEM((1, ROWS), jnp.int32),
    "home": pltpu.SMEM((1, BLOCKS), jnp.int32),
    "input_gain": pltpu.VMEM((1, WIDTH), jnp.float32),
    "q_gain": pltpu.VMEM((1, HEAD), jnp.float32),
    "k_gain": pltpu.VMEM((1, HEAD), jnp.float32),
    "cosine": pltpu.VMEM((ROWS, HEAD), jnp.float32),
    "sine": pltpu.VMEM((ROWS, HEAD), jnp.float32),
    "bias": pltpu.VMEM((ROWS, BAND), jnp.float32),
    "keys": pltpu.VMEM((ROWS, HEAD), jnp.bfloat16),
    "values": pltpu.VMEM((ROWS, HEAD), jnp.bfloat16),
    "queries": pltpu.VMEM((2, ROWS, HEAD), jnp.bfloat16),
    "partial": pltpu.VMEM((ROWS, 2 * HEAD), jnp.float32),
    "context": pltpu.VMEM((BLOCKS, BLK, HEAD), jnp.bfloat16),
    "send": pltpu.VMEM((HEADS, SEQ, OWN, HEAD), jnp.bfloat16),
    "small": pltpu.SemaphoreType.DMA((6,)),
    "own": pltpu.SemaphoreType.DMA((CHUNKS,)),
    "weight_send": pltpu.SemaphoreType.DMA((CHUNKS,)),
    "weight_recv": pltpu.SemaphoreType.DMA((CHUNKS, 5)),
    "row_send": pltpu.SemaphoreType.DMA,
    "row_recv": pltpu.SemaphoreType.DMA((3,)),
    "twin_send": pltpu.SemaphoreType.DMA,
    "twin_recv": pltpu.SemaphoreType.DMA((4,)),
    "context_send": pltpu.SemaphoreType.DMA,
    "context_recv": pltpu.SemaphoreType.DMA,
    "context_own": pltpu.SemaphoreType.DMA,
}
OPERANDS = (
    "hidden",
    "segments_in",
    "home_in",
    "input_gain_in",
    "q_gain_in",
    "k_gain_in",
    "w_query",
    "key_weight",
    "value_weight",
    "out",
)


def kernel(*refs):
    b = Buffers(OPERANDS + tuple(SCRATCH), refs)
    small = [
        pltpu.make_async_copy(src, dst, b.small.at[i])
        for i, (src, dst) in enumerate(
            (
                (b.hidden.at[0], b.hidden_here),
                (b.input_gain_in, b.input_gain),
                (b.segments_in, b.segments),
                (b.home_in, b.home),
                (b.q_gain_in, b.q_gain),
                (b.k_gain_in, b.k_gain),
            )
        )
    ]
    for j in range(CHUNKS):
        begin_own(b, j)
        if j == 0:
            for copy in small:
                copy.start()
    barrier()

    for j in range(CHUNKS):
        finish_own(b, j)
        begin_first(b, j)
    small[0].wait()
    small[1].wait()
    normalize(b)
    begin_rows(b)
    for copy in small[2:]:
        copy.wait()
    tables(b)
    for j in range(CHUNKS):
        pass_first(b, j)
    begin_second(b, 0, 0)
    begin_second(b, 0, 1)
    begin_second(b, 1, 0)
    rows_arrived(b, 0)
    pass_second(b, 0)
    pass_second(b, 1)
    rows_arrived(b, 1)

    for part in (3, 4):
        arrived(b, b.wide.at[0, pl.ds(0, 8)], b.weight_recv.at[0, part])
    for group in (3, 0, 1):
        twin_arrived(b, group)

    @pl.loop(0, SIDE - 1)
    def _(k):
        project_keys(b, chip_rows((k + 3) % SIDE))

    pass_second(b, 2)
    for part in (3, 4):
        arrived(b, b.wide.at[1, pl.ds(0, 8)], b.weight_recv.at[1, part])

    @pl.loop(0, SIDE - 1)
    def _(k):
        project_queries(b, chip_rows((k + 3) % SIDE))

    rows_arrived(b, 2)
    twin_arrived(b, 2)
    project_keys(b, chip_rows(2))
    project_queries(b, chip_rows(2))

    @pl.loop(0, 2)
    def _(h):
        attend(b, h, h)

    @pl.loop(2, WIDE_CHUNKS)
    def _(j):
        arrived(b, b.wide.at[j, pl.ds(0, 8)], b.weight_recv.at[j, 3])
        project_early(b, b.wide.at[j])

        @pl.when(j == 2)
        def _():
            pass_second(b, 3)

        @pl.when(j == 3)
        def _():
            pass_second(b, 4)

        arrived(b, b.wide.at[j, pl.ds(0, 8)], b.weight_recv.at[j, 4])
        project_late(b, b.wide.at[j])

        @pl.loop(0, 2)
        def _(h):
            attend(b, h, 2 * (j - 1) + h)

    @pl.loop(0, NARROW_CHUNKS)
    def _(n):
        arrived(b, b.narrow.at[n, pl.ds(0, 8)], b.weight_recv.at[WIDE_CHUNKS + n, 3])
        project_early(b, b.narrow.at[n])

        @pl.when(n == 0)
        def _():
            pass_second(b, 5)

        arrived(b, b.narrow.at[n, pl.ds(0, 8)], b.weight_recv.at[WIDE_CHUNKS + n, 4])
        project_late(b, b.narrow.at[n])
        attend(b, 0, 2 * (WIDE_CHUNKS - 1) + n)

    for j in range(CHUNKS):
        left(b, chunk(b, j).at[pl.ds(0, PIECES - 2)], b.weight_send.at[j])
    left(b, b.rows.at[pl.ds(0, 6 * PIECE)], b.row_send)
    left(b, b.rows.at[pl.ds(0, OWN + 6 * PIECE)], b.twin_send)
    finish_context(b)


def hand_over(src, dst, sems):
    part = OWN // 4
    copies = [
        pltpu.make_async_copy(src.at[:, pl.ds(i * part, part)], dst.at[:, pl.ds(i * part, part)], sems.at[i])
        for i in range(4)
    ]
    for copy in copies:
        copy.start()
    for copy in copies:
        copy.wait()


def body(hidden_rows, segment_ids, block_home, input_gain, w_query, key_weight, value_weight, q_gain, k_gain):
    anywhere = pl.BlockSpec(memory_space=pl.ANY)
    vector = pl.BlockSpec(memory_space=pltpu.VMEM)
    shape = (1, OWN, SEQ * HEADS * HEAD)
    moved = pl.pallas_call(
        kernel,
        out_shape=pltpu.VMEM(shape, jnp.bfloat16),
        in_specs=[anywhere] * 9,
        out_specs=vector,
        scratch_shapes=list(SCRATCH.values()),
        compiler_params=pltpu.CompilerParams(
            collective_id=0, has_side_effects=True, vmem_limit_bytes=52 * 1024 * 1024
        ),
        name="packed_attention",
    )(
        hidden_rows,
        segment_ids,
        block_home,
        input_gain.reshape(1, WIDTH),
        q_gain.reshape(1, HEAD),
        k_gain.reshape(1, HEAD),
        w_query.reshape(2, HALF, HEADS * HEAD),
        key_weight.reshape(2, HALF, HEAD),
        value_weight.reshape(2, HALF, HEAD),
    )
    return pl.pallas_call(
        hand_over,
        out_shape=jax.ShapeDtypeStruct(shape, jnp.bfloat16),
        in_specs=[vector],
        out_specs=anywhere,
        scratch_shapes=[pltpu.SemaphoreType.DMA((4,))],
        compiler_params=pltpu.CompilerParams(vmem_limit_bytes=4 * 1024 * 1024),
        name="hand_over",
    )(moved)


def solution(mesh):
    return jax.shard_map(
        body,
        mesh=mesh,
        in_specs=(
            P("dp", "seq", None),
            P("dp", None),
            P("dp", None),
            P(),
            P("dp", "seq"),
            P("dp", "seq"),
            P("dp", "seq"),
            P(),
            P(),
        ),
        out_specs=P("dp", "seq", None),
        check_vma=False,
    )
```

time: 103 us -> 89.3 us (0.87)
  Pallas kernels: 99.4 us -> 89 us
  local copies, waits for them, and re-layouts: 3.1 us -> 0 us
    pallas_call x1 -> x2, Pallas kernels: 99.4 us -> 89 us  [the longest x1 87.7 us: body(): pl.pallas_call(kernel, out_shape=pltpu.VMEM(shape, jnp.bfloat16), in_spec...]
    unnamed x1 -> x0, local copies, waits for them, and re-layouts: 3.1 us -> none
where the time goes in v2:
time: 89.3 us; the launch traced here: 89.2 us
  Pallas kernels  89 us (100%)
    pallas_call x1, Pallas kernels, body(): pl.pallas_call(kernel, out_shape=pltpu.VMEM(shape, jnp.bfloat16), in_spec...  87.7 us

profile of v2, /device:TPU:1, one launch (start us, length us, event | category | flops | bytes accessed | tf_op | source)
XLA Modules:
  0.0 89.2 jit_solution(11002688117905344711)
XLA Ops:
  0.0 87.7 %packed_attention.1.src = bf16[1,128,8192]{2,1,0:T(8,128)(2,1)S(1)} custom-call(bf16[1,128,5120]{2,1,0:T(8,128)(2,1)} %refs_0_.1, s32[1,1024]{1,0:T(1,128)} %refs_1_.1, s32[1,64]{1,0:T(1,128)} %refs_2_.1, f32[1,5120]{1,0:T(1,128)} %bitcast.9, f32[1,128]{1,0:T(1,128)} %bitcast.10, f32[1,128]{1,0:T(1,128)} %bitcast.11, bf16[2,160,1024]{2,1,0:T(8,128)(2,1)} %bitcast.6, ...), custom_call_target="tpu_custom_call" | custom-call | tf_op jit(solution)/shard_map/packed_attention/pallas_call | solution.py:516
  87.7 1.3 %hand_over.1 = bf16[1,128,8192]{2,1,0:T(8,128)(2,1)} custom-call(bf16[1,128,8192]{2,1,0:T(8,128)(2,1)S(1)} %packed_attention.1.src), custom_call_target="tpu_custom_call" | custom-call | tf_op jit(solution)/shard_map/hand_over/pallas_call | solution.py:537

commit v3 on v2

--- a/solution.py
+++ b/solution.py
@@ -62,7 +62,9 @@
 
 
 def chunk(b, j):
-    return b.wide.at[j] if j < WIDE_CHUNKS else b.narrow.at[j - WIDE_CHUNKS]
+    if j < WIDE_CHUNKS:
+        return b.wide.at[j]
+    return b.wide.at[WIDE_CHUNKS, :, :, pl.ds((j - WIDE_CHUNKS) * HEAD, HEAD)]
 
 
 def arrived(b, view, sem):
@@ -113,9 +115,11 @@
         first_send(b, j, kind)
 
 
+def finish_first(b, j):
+    arrived(b, chunk(b, j).at[pl.ds(0, 2)], b.weight_recv.at[j, 1])
+
+
 def begin_second(b, j, part):
-    if part == 0:
-        arrived(b, chunk(b, j).at[pl.ds(0, 2)], b.weight_recv.at[j, 1])
     for kind in ((0, 3), (1, 4))[part]:
         second_send(b, j, kind)
 
@@ -128,6 +132,10 @@
         begin_second(b, j + 1, 1)
     if j + 2 < CHUNKS:
         begin_second(b, j + 2, 0)
+
+
+def finish_second(b, j, part):
+    arrived(b, chunk(b, j).at[pl.ds(0, 8)], b.weight_recv.at[j, 3 + part])
 
 
 def rows_of(b, owner, part):
@@ -161,9 +169,12 @@
     arrived(b, b.rows.at[pl.ds(0, OWN)], b.twin_recv.at[group])
 
 
-def begin_rows(b):
+def begin_rows(b, part):
     s, d, _, _ = place()
-    for kind in (0, 3, 1, 4):
+    if part == 0:
+        row_send(b, 0)
+        return
+    for kind in (3, 1, 4):
         row_send(b, kind)
     twin = s + 1 - 2 * (s % 2)
     view = rows_of(b, s, None)
@@ -204,10 +215,10 @@
     pltpu.make_async_copy(view, view, b.own.at[j]).wait()
 
 
-def normalize(b):
+def normalize(b, part):
     s, _, _, _ = place()
 
-    @pl.loop(0, OWN // BLK)
+    @pl.loop(part * PIECE // BLK, (part + 1) * PIECE // BLK)
     def _(i):
         at = pl.multiple_of(i * BLK, BLK)
         wide = b.hidden_here[pl.ds(at, BLK), :].astype(jnp.float32)
@@ -275,16 +286,19 @@
         b.queries[h, at, :] = turned(b, raw[:, h * HEAD : (h + 1) * HEAD], b.q_gain[...], at)
 
 
-def project_queries(b, at):
-    raw = jnp.dot(b.rows[at, :], b.wide.at[1].reshape(WIDTH, 2 * HEAD)[...], preferred_element_type=jnp.float32)
+def project_queries(b, j, at):
+    raw = jnp.dot(b.rows[at, :], b.wide.at[j].reshape(WIDTH, 2 * HEAD)[...], preferred_element_type=jnp.float32)
     keep_queries(b, raw, at)
 
 
-def lines_product(b, piece, at, late):
+FIRST_LINES, NEXT_LINES, LAST_LINES = (0,), (1, 3), (2,)
+
+
+def lines_product(b, piece, at, steps):
     _, _, x, y = place()
     left_sides, right_sides = [], []
     for half, mine in ((0, y), (1, x)):
-        for step in (2,) if late else (0, 1, 3):
+        for step in steps:
             line = half * SIDE + (mine + step) % SIDE
             left_sides.append(b.rows[at, pl.ds(pl.multiple_of(line * LINE, HEAD), LINE)])
             right_sides.append(piece[pl.ds(line * SIDE, SIDE)].reshape(LINE, piece.shape[-1]))
@@ -293,38 +307,63 @@
     )
 
 
-def project_early(b, piece):
-    columns = pl.ds(0, piece.shape[-1])
+def project_early(b, piece, partial):
+    for k in (3, 0, 1):
+        at = chip_rows(k)
+        partial[at, :] += lines_product(b, piece, at, NEXT_LINES)
+    at = chip_rows(2)
+    partial[at, :] = lines_product(b, piece, at, FIRST_LINES + NEXT_LINES)
+
+
+def attend(b, heads, head, query):
+    steps = ROWS // QROWS
+
+    def reach_of(i):
+        reach = min((i + 1) * QROWS, BAND)
+        return reach, pl.ds((i + 1) * QROWS - reach, reach)
+
+    def score(i):
+        keys = b.keys[reach_of(i)[1], :]
+        return lax.dot_general(query(i), keys, (((1,), (1,)), ((), ())), preferred_element_type=jnp.float32)
+
+    def mix(i, scores):
+        reach, keys = reach_of(i)
+        bias = b.bias[pl.ds(i * QROWS, QROWS), BAND - reach :]
+        weights = jnp.exp2(scores.reshape(heads, QROWS, reach) * SCALE + bias[None]).reshape(heads * QROWS, reach)
+        total = jnp.sum(weights, axis=1, keepdims=True)
+        mixed = jnp.dot(weights.astype(jnp.bfloat16), b.values[keys, :], preferred_element_type=jnp.float32)
+        context = (mixed / total).astype(jnp.bfloat16).reshape(heads, QROWS // BLK, BLK, HEAD)
+        for h in range(heads):
+            b.context[h, pl.ds(i * (QROWS // BLK), QROWS // BLK)] = context[h]
+
+    scores = score(0)
+    for i in range(steps):
+        later = score(i + 1) if i + 1 < steps else None
+        mix(i, scores)
+        scores = later
+
+    per = BLOCKS // SEQ
+    for h in range(heads):
+        for t in range(SEQ):
+            for r in range(per):
+                b.send[head + h, t, pl.ds(r * BLK, BLK), :] = b.context[h, b.home[0, t * per + r]]
+        send_context(b, head + h)
+
+
+def attend_kept(b, heads, head):
+    def query(i):
+        at = pl.ds(i * QROWS, QROWS)
+        if heads == 1:
+            return b.queries[0, at, :]
+        return jnp.concatenate([b.queries[h, at, :] for h in range(heads)], axis=0)
+
+    attend(b, heads, head, query)
+
+
+def project_late(b, piece, partial):
     for i in range(ROWS // QROWS):
         at = pl.ds(i * QROWS, QROWS)
-        b.partial[at, columns] = lines_product(b, piece, at, False)
-
-
-def project_late(b, piece):
-    columns = pl.ds(0, piece.shape[-1])
-    for i in range(ROWS // QROWS):
-        at = pl.ds(i * QROWS, QROWS)
-        keep_queries(b, b.partial[at, columns] + lines_product(b, piece, at, True), at)
-
-
-def attend(b, slot, head):
-    for i in range(ROWS // QROWS):
-        reach = min((i + 1) * QROWS, BAND)
-        keys = pl.ds((i + 1) * QROWS - reach, reach)
-        at = pl.ds(i * QROWS, QROWS)
-        scores = lax.dot_general(
-            b.queries[slot, at, :], b.keys[keys, :], (((1,), (1,)), ((), ())), preferred_element_type=jnp.float32
-        )
-        weights = jnp.exp2(scores * SCALE + b.bias[at, BAND - reach :])
-        total = jnp.sum(weights, axis=1, keepdims=True)
-        mixed = jnp.dot(weights.astype(jnp.bfloat16), b.values[keys, :], preferred_element_type=jnp.float32)
-        context = (mixed / total).astype(jnp.bfloat16)
-        b.context[pl.ds(i * (QROWS // BLK), QROWS // BLK)] = context.reshape(QROWS // BLK, BLK, HEAD)
-    per = BLOCKS // SEQ
-    for t in range(SEQ):
-        for r in range(per):
-            b.send[head, t, pl.ds(r * BLK, BLK), :] = b.context[b.home[0, t * per + r]]
-    send_context(b, head)
+        keep_queries(b, partial[at, :] + lines_product(b, piece, at, LAST_LINES), at)
 
 
 def barrier():
@@ -346,8 +385,7 @@
 
 SCRATCH = {
     "rows": pltpu.VMEM((ROWS, WIDTH), jnp.bfloat16),
-    "wide": pltpu.VMEM((WIDE_CHUNKS, PIECES, HALF, 2 * HEAD), jnp.bfloat16),
-    "narrow": pltpu.VMEM((NARROW_CHUNKS, PIECES, HALF, HEAD), jnp.bfloat16),
+    "wide": pltpu.VMEM((WIDE_CHUNKS + 1, PIECES, HALF, 2 * HEAD), jnp.bfloat16),
     "hidden_here": pltpu.VMEM((OWN, WIDTH), jnp.bfloat16),
     "segments": pltpu.VMEM((1, ROWS), jnp.int32),
     "home": pltpu.SMEM((1, BLOCKS), jnp.int32),
@@ -360,8 +398,8 @@
     "keys": pltpu.VMEM((ROWS, HEAD), jnp.bfloat16),
     "values": pltpu.VMEM((ROWS, HEAD), jnp.bfloat16),
     "queries": pltpu.VMEM((2, ROWS, HEAD), jnp.bfloat16),
-    "partial": pltpu.VMEM((ROWS, 2 * HEAD), jnp.float32),
-    "context": pltpu.VMEM((BLOCKS, BLK, HEAD), jnp.bfloat16),
+    "partial": pltpu.VMEM((WIDE_CHUNKS - 1, ROWS, 2 * HEAD), jnp.float32),
+    "context": pltpu.VMEM((2, BLOCKS, BLK, HEAD), jnp.bfloat16),
     "send": pltpu.VMEM((HEADS, SEQ, OWN, HEAD), jnp.bfloat16),
     "small": pltpu.SemaphoreType.DMA((6,)),
     "own": pltpu.SemaphoreType.DMA((CHUNKS,)),
@@ -416,79 +454,83 @@
         begin_first(b, j)
     small[0].wait()
     small[1].wait()
-    normalize(b)
-    begin_rows(b)
+    for part in range(2):
+        normalize(b, part)
+        begin_rows(b, part)
     for copy in small[2:]:
         copy.wait()
     tables(b)
     for j in range(CHUNKS):
         pass_first(b, j)
+    finish_first(b, 0)
     begin_second(b, 0, 0)
     begin_second(b, 0, 1)
+    finish_first(b, 1)
     begin_second(b, 1, 0)
+    for j in range(2, CHUNKS):
+        finish_first(b, j)
     rows_arrived(b, 0)
     pass_second(b, 0)
     pass_second(b, 1)
     rows_arrived(b, 1)
 
-    for part in (3, 4):
-        arrived(b, b.wide.at[0, pl.ds(0, 8)], b.weight_recv.at[0, part])
+    for part in range(2):
+        finish_second(b, 0, part)
     for group in (3, 0, 1):
         twin_arrived(b, group)
 
     @pl.loop(0, SIDE - 1)
     def _(k):
-        project_keys(b, chip_rows((k + 3) % SIDE))
+        at = chip_rows((k + 3) % SIDE)
+        project_keys(b, at)
+        for j in (3, 4):
+            b.partial[j - 2, at, :] = lines_product(b, b.wide.at[j], at, FIRST_LINES)
 
     pass_second(b, 2)
-    for part in (3, 4):
-        arrived(b, b.wide.at[1, pl.ds(0, 8)], b.weight_recv.at[1, part])
+    for part in range(2):
+        finish_second(b, 1, part)
 
     @pl.loop(0, SIDE - 1)
     def _(k):
-        project_queries(b, chip_rows((k + 3) % SIDE))
+        project_queries(b, 1, chip_rows((k + 3) % SIDE))
+
+    finish_second(b, 2, 0)
+
+    @pl.loop(0, SIDE - 1)
+    def _(k):
+        at = chip_rows((k + 3) % SIDE)
+        b.partial[0, at, :] = lines_product(b, b.wide.at[2], at, FIRST_LINES + NEXT_LINES)
 
     rows_arrived(b, 2)
     twin_arrived(b, 2)
     project_keys(b, chip_rows(2))
-    project_queries(b, chip_rows(2))
-
-    @pl.loop(0, 2)
-    def _(h):
-        attend(b, h, h)
-
-    @pl.loop(2, WIDE_CHUNKS)
-    def _(j):
-        arrived(b, b.wide.at[j, pl.ds(0, 8)], b.weight_recv.at[j, 3])
-        project_early(b, b.wide.at[j])
-
-        @pl.when(j == 2)
-        def _():
-            pass_second(b, 3)
-
-        @pl.when(j == 3)
-        def _():
-            pass_second(b, 4)
-
-        arrived(b, b.wide.at[j, pl.ds(0, 8)], b.weight_recv.at[j, 4])
-        project_late(b, b.wide.at[j])
-
-        @pl.loop(0, 2)
-        def _(h):
-            attend(b, h, 2 * (j - 1) + h)
-
-    @pl.loop(0, NARROW_CHUNKS)
-    def _(n):
-        arrived(b, b.narrow.at[n, pl.ds(0, 8)], b.weight_recv.at[WIDE_CHUNKS + n, 3])
-        project_early(b, b.narrow.at[n])
-
-        @pl.when(n == 0)
-        def _():
-            pass_second(b, 5)
-
-        arrived(b, b.narrow.at[n, pl.ds(0, 8)], b.weight_recv.at[WIDE_CHUNKS + n, 4])
-        project_late(b, b.narrow.at[n])
-        attend(b, 0, 2 * (WIDE_CHUNKS - 1) + n)
+    project_queries(b, 1, chip_rows(2))
+    attend_kept(b, 2, 0)
+
+    pass_second(b, 3)
+    finish_second(b, 2, 1)
+    for k in (3, 0, 1):
+        at = chip_rows(k)
+        keep_queries(b, b.partial[0, at, :] + lines_product(b, b.wide.at[2], at, LAST_LINES), at)
+    project_queries(b, 2, chip_rows(2))
+    attend_kept(b, 2, 2)
+
+    finish_second(b, 3, 0)
+    project_early(b, b.wide.at[3], b.partial.at[1])
+    pass_second(b, 4)
+    finish_second(b, 3, 1)
+    project_late(b, b.wide.at[3], b.partial.at[1])
+    attend_kept(b, 2, 4)
+
+    for j in range(WIDE_CHUNKS, CHUNKS):
+        finish_second(b, j, 0)
+        partial = b.partial.at[2, :, pl.ds((j - WIDE_CHUNKS) * HEAD, HEAD)]
+        project_early(b, chunk(b, j), partial)
+        if j + 1 < CHUNKS:
+            pass_second(b, j + 1)
+        finish_second(b, j, 1)
+        project_late(b, chunk(b, j), partial)
+        attend_kept(b, 1, j + 2)
 
     for j in range(CHUNKS):
         left(b, chunk(b, j).at[pl.ds(0, PIECES - 2)], b.weight_send.at[j])

time: 89.3 us -> 87 us (0.974)
  Pallas kernels: 89 us -> 86.8 us
    pallas_call x1, Pallas kernels: 87.7 us -> 85.4 us  [body(): pl.pallas_call(kernel, out_shape=pltpu.VMEM(shape, jnp.bfloat16), in_spec...]
where the time goes in v3:
time: 87 us; the launch traced here: 86.9 us
  Pallas kernels  86.8 us (100%)
    pallas_call x1, Pallas kernels, body(): pl.pallas_call(kernel, out_shape=pltpu.VMEM(shape, jnp.bfloat16), in_spec...  85.4 us

profile of v3, /device:TPU:1, one launch (start us, length us, event | category | flops | bytes accessed | tf_op | source)
XLA Modules:
  0.0 86.9 jit_solution(17859545105474665885)
XLA Ops:
  0.0 85.4 %packed_attention.1.src = bf16[1,128,8192]{2,1,0:T(8,128)(2,1)S(1)} custom-call(bf16[1,128,5120]{2,1,0:T(8,128)(2,1)} %refs_0_.1, s32[1,1024]{1,0:T(1,128)} %refs_1_.1, s32[1,64]{1,0:T(1,128)} %refs_2_.1, f32[1,5120]{1,0:T(1,128)} %bitcast.9, f32[1,128]{1,0:T(1,128)} %bitcast.10, f32[1,128]{1,0:T(1,128)} %bitcast.11, bf16[2,160,1024]{2,1,0:T(8,128)(2,1)} %bitcast.6, ...), custom_call_target="tpu_custom_call" | custom-call | tf_op jit(solution)/shard_map/packed_attention/pallas_call | solution.py:558
  85.4 1.3 %hand_over.1 = bf16[1,128,8192]{2,1,0:T(8,128)(2,1)} custom-call(bf16[1,128,8192]{2,1,0:T(8,128)(2,1)S(1)} %packed_attention.1.src), custom_call_target="tpu_custom_call" | custom-call | tf_op jit(solution)/shard_map/hand_over/pallas_call | solution.py:579

commit v4 on v3

--- a/solution.py
+++ b/solution.py
@@ -16,6 +16,7 @@
 ROWS = 1024
 OWN = ROWS // SEQ
 PIECE = OWN // 2
+TAIL = 16
 WIDTH = 5120
 SHARD = WIDTH // (SIDE * SIDE)
 HALF = SHARD // 2
@@ -138,47 +139,53 @@
     arrived(b, chunk(b, j).at[pl.ds(0, 8)], b.weight_recv.at[j, 3 + part])
 
 
-def rows_of(b, owner, part):
-    if part is None:
-        return b.rows.at[pl.ds(pl.multiple_of(owner * OWN, OWN), OWN)]
-    return b.rows.at[pl.ds(pl.multiple_of(owner * OWN + part * PIECE, PIECE), PIECE)]
-
-
-def row_send(b, kind):
+GROUPS = (((0, 3), 0, PIECE), ((1, 4), 0, PIECE), ((2, 5), 0, PIECE - TAIL), ((2, 5), PIECE - TAIL, TAIL))
+
+
+def rows_of(b, owner, part, group):
+    _, start, size = GROUPS[group]
+    return b.rows.at[pl.ds(pl.multiple_of(owner * OWN + part * PIECE + start, TAIL), size)]
+
+
+def row_send(b, kind, group):
     s, d, _, _ = place()
     whose, part, way = SECOND[kind]
-    view = rows_of(b, (s + 2 * whose + SEQ) % SEQ, part)
-    target = (s + 2 * way + SEQ) % SEQ
-    remote(view, view, b.row_send, b.row_recv.at[{0: 0, 3: 0, 1: 1, 4: 1, 2: 2, 5: 2}[kind]], target, d).start()
+    view = rows_of(b, (s + 2 * whose + SEQ) % SEQ, part, group)
+    remote(view, view, b.row_send, b.row_recv.at[group], (s + 2 * way + SEQ) % SEQ, d).start()
 
 
 def rows_arrived(b, group):
     s, d, _, _ = place()
-    arrived(b, b.rows.at[pl.ds(0, OWN)], b.row_recv.at[group])
+    kinds, _, size = GROUPS[group]
+    arrived(b, b.rows.at[pl.ds(0, 2 * size)], b.row_recv.at[group])
     if group == 0:
-        for kind in (2, 5):
-            row_send(b, kind)
+        for onward in (2, 3):
+            for kind in GROUPS[onward][0]:
+                row_send(b, kind, onward)
     twin = s + 1 - 2 * (s % 2)
-    for kind in ((0, 3), (1, 4), (2, 5))[group]:
+    for kind in kinds:
         whose, part, way = SECOND[kind]
-        view = rows_of(b, (s + 2 * (whose - way) + SEQ) % SEQ, part)
+        view = rows_of(b, (s + 2 * (whose - way) + SEQ) % SEQ, part, group)
         remote(view, view, b.twin_send, b.twin_recv.at[group], twin, d).start()
 
 
 def twin_arrived(b, group):
-    arrived(b, b.rows.at[pl.ds(0, OWN)], b.twin_recv.at[group])
-
-
-def begin_rows(b, part):
+    size = PIECE if group == len(GROUPS) else GROUPS[group][2]
+    arrived(b, b.rows.at[pl.ds(0, 2 * size)], b.twin_recv.at[group])
+
+
+def begin_rows(b):
     s, d, _, _ = place()
-    if part == 0:
-        row_send(b, 0)
-        return
-    for kind in (3, 1, 4):
-        row_send(b, kind)
+    up, down = (s + 2) % SEQ, (s + SEQ - 2) % SEQ
+    for start, target in ((0, up), (PIECE, down), (PIECE // 2, up), (PIECE + PIECE // 2, down)):
+        normalize(b, start)
+        view = b.rows.at[pl.ds(pl.multiple_of(s * OWN + start, PIECE // 2), PIECE // 2)]
+        remote(view, view, b.row_send, b.row_recv.at[0], target, d).start()
+    row_send(b, 1, 1)
+    row_send(b, 4, 1)
     twin = s + 1 - 2 * (s % 2)
-    view = rows_of(b, s, None)
-    remote(view, view, b.twin_send, b.twin_recv.at[3], twin, d).start()
+    view = b.rows.at[pl.ds(pl.multiple_of(s * OWN, OWN), OWN)]
+    remote(view, view, b.twin_send, b.twin_recv.at[len(GROUPS)], twin, d).start()
 
 
 def send_context(b, head):
@@ -215,10 +222,10 @@
     pltpu.make_async_copy(view, view, b.own.at[j]).wait()
 
 
-def normalize(b, part):
+def normalize(b, start):
     s, _, _, _ = place()
 
-    @pl.loop(part * PIECE // BLK, (part + 1) * PIECE // BLK)
+    @pl.loop(start // BLK, (start + PIECE // 2) // BLK)
     def _(i):
         at = pl.multiple_of(i * BLK, BLK)
         wide = b.hidden_here[pl.ds(at, BLK), :].astype(jnp.float32)
@@ -308,11 +315,9 @@
 
 
 def project_early(b, piece, partial):
-    for k in (3, 0, 1):
-        at = chip_rows(k)
+    for i in range(ROWS // QROWS):
+        at = pl.ds(i * QROWS, QROWS)
         partial[at, :] += lines_product(b, piece, at, NEXT_LINES)
-    at = chip_rows(2)
-    partial[at, :] = lines_product(b, piece, at, FIRST_LINES + NEXT_LINES)
 
 
 def attend(b, heads, head, query):
@@ -350,14 +355,13 @@
         send_context(b, head + h)
 
 
-def attend_kept(b, heads, head):
+def attend_kept(b, head, slots):
     def query(i):
         at = pl.ds(i * QROWS, QROWS)
-        if heads == 1:
-            return b.queries[0, at, :]
-        return jnp.concatenate([b.queries[h, at, :] for h in range(heads)], axis=0)
-
-    attend(b, heads, head, query)
+        parts = [b.queries[slot, at, :] for slot in slots]
+        return parts[0] if len(parts) == 1 else jnp.concatenate(parts, axis=0)
+
+    attend(b, len(slots), head, query)
 
 
 def project_late(b, piece, partial):
@@ -406,9 +410,9 @@
     "weight_send": pltpu.SemaphoreType.DMA((CHUNKS,)),
     "weight_recv": pltpu.SemaphoreType.DMA((CHUNKS, 5)),
     "row_send": pltpu.SemaphoreType.DMA,
-    "row_recv": pltpu.SemaphoreType.DMA((3,)),
+    "row_recv": pltpu.SemaphoreType.DMA((len(GROUPS),)),
     "twin_send": pltpu.SemaphoreType.DMA,
-    "twin_recv": pltpu.SemaphoreType.DMA((4,)),
+    "twin_recv": pltpu.SemaphoreType.DMA((len(GROUPS) + 1,)),
     "context_send": pltpu.SemaphoreType.DMA,
     "context_recv": pltpu.SemaphoreType.DMA,
     "context_own": pltpu.SemaphoreType.DMA,
@@ -449,14 +453,15 @@
                 copy.start()
     barrier()
 
-    for j in range(CHUNKS):
+    for j in range(2):
         finish_own(b, j)
         begin_first(b, j)
     small[0].wait()
     small[1].wait()
-    for part in range(2):
-        normalize(b, part)
-        begin_rows(b, part)
+    begin_rows(b)
+    for j in range(2, CHUNKS):
+        finish_own(b, j)
+        begin_first(b, j)
     for copy in small[2:]:
         copy.wait()
     tables(b)
@@ -476,7 +481,7 @@
 
     for part in range(2):
         finish_second(b, 0, part)
-    for group in (3, 0, 1):
+    for group in (len(GROUPS), 0, 1):
         twin_arrived(b, group)
 
     @pl.loop(0, SIDE - 1)
@@ -501,11 +506,14 @@
         at = chip_rows((k + 3) % SIDE)
         b.partial[0, at, :] = lines_product(b, b.wide.at[2], at, FIRST_LINES + NEXT_LINES)
 
-    rows_arrived(b, 2)
-    twin_arrived(b, 2)
+    for group in (2, 3):
+        rows_arrived(b, group)
+    for group in (2, 3):
+        twin_arrived(b, group)
     project_keys(b, chip_rows(2))
     project_queries(b, 1, chip_rows(2))
-    attend_kept(b, 2, 0)
+    attend_kept(b, 0, (0,))
+    attend_kept(b, 1, (1,))
 
     pass_second(b, 3)
     finish_second(b, 2, 1)
@@ -513,14 +521,17 @@
         at = chip_rows(k)
         keep_queries(b, b.partial[0, at, :] + lines_product(b, b.wide.at[2], at, LAST_LINES), at)
     project_queries(b, 2, chip_rows(2))
-    attend_kept(b, 2, 2)
+    attend_kept(b, 2, (0, 1))
+    for j in (3, 4):
+        at = chip_rows(2)
+        b.partial[j - 2, at, :] = lines_product(b, b.wide.at[j], at, FIRST_LINES)
 
     finish_second(b, 3, 0)
     project_early(b, b.wide.at[3], b.partial.at[1])
     pass_second(b, 4)
     finish_second(b, 3, 1)
     project_late(b, b.wide.at[3], b.partial.at[1])
-    attend_kept(b, 2, 4)
+    attend_kept(b, 4, (0, 1))
 
     for j in range(WIDE_CHUNKS, CHUNKS):
         finish_second(b, j, 0)
@@ -530,7 +541,7 @@
             pass_second(b, j + 1)
         finish_second(b, j, 1)
         project_late(b, chunk(b, j), partial)
-        attend_kept(b, 1, j + 2)
+        attend_kept(b, j + 2, (0,))
 
     for j in range(CHUNKS):
         left(b, chunk(b, j).at[pl.ds(0, PIECES - 2)], b.weight_send.at[j])

time: 87 us -> 86.1 us (0.990)
  Pallas kernels: 86.8 us -> 85.9 us
    pallas_call x1, Pallas kernels: 85.4 us -> 84.5 us  [body(): pl.pallas_call(kernel, out_shape=pltpu.VMEM(shape, jnp.bfloat16), in_spec...]
where the time goes in v4:
time: 86.1 us; the launch traced here: 86 us
  Pallas kernels  85.9 us (100%)
    pallas_call x1, Pallas kernels, body(): pl.pallas_call(kernel, out_shape=pltpu.VMEM(shape, jnp.bfloat16), in_spec...  84.5 us

profile of v4, /device:TPU:1, one launch (start us, length us, event | category | flops | bytes accessed | tf_op | source)
XLA Modules:
  0.0 86.0 jit_solution(2775048303008712613)
XLA Ops:
  0.0 84.5 %packed_attention.1.src = bf16[1,128,8192]{2,1,0:T(8,128)(2,1)S(1)} custom-call(bf16[1,128,5120]{2,1,0:T(8,128)(2,1)} %refs_0_.1, s32[1,1024]{1,0:T(1,128)} %refs_1_.1, s32[1,64]{1,0:T(1,128)} %refs_2_.1, f32[1,5120]{1,0:T(1,128)} %bitcast.9, f32[1,128]{1,0:T(1,128)} %bitcast.10, f32[1,128]{1,0:T(1,128)} %bitcast.11, bf16[2,160,1024]{2,1,0:T(8,128)(2,1)} %bitcast.6, ...), custom_call_target="tpu_custom_call" | custom-call | tf_op jit(solution)/shard_map/packed_attention/pallas_call | solution.py:569
  84.5 1.3 %hand_over.1 = bf16[1,128,8192]{2,1,0:T(8,128)(2,1)} custom-call(bf16[1,128,8192]{2,1,0:T(8,128)(2,1)S(1)} %packed_attention.1.src), custom_call_target="tpu_custom_call" | custom-call | tf_op jit(solution)/shard_map/hand_over/pallas_call | solution.py:590

commit v5 on v4

--- a/solution.py
+++ b/solution.py
@@ -512,8 +512,10 @@
         twin_arrived(b, group)
     project_keys(b, chip_rows(2))
     project_queries(b, 1, chip_rows(2))
-    attend_kept(b, 0, (0,))
-    attend_kept(b, 1, (1,))
+
+    @pl.loop(0, 2)
+    def _(h):
+        attend_kept(b, h, (h,))
 
     pass_second(b, 3)
     finish_second(b, 2, 1)
@@ -533,15 +535,20 @@
     project_late(b, b.wide.at[3], b.partial.at[1])
     attend_kept(b, 4, (0, 1))
 
-    for j in range(WIDE_CHUNKS, CHUNKS):
-        finish_second(b, j, 0)
-        partial = b.partial.at[2, :, pl.ds((j - WIDE_CHUNKS) * HEAD, HEAD)]
-        project_early(b, chunk(b, j), partial)
-        if j + 1 < CHUNKS:
-            pass_second(b, j + 1)
-        finish_second(b, j, 1)
-        project_late(b, chunk(b, j), partial)
-        attend_kept(b, j + 2, (0,))
+    @pl.loop(0, NARROW_CHUNKS)
+    def _(n):
+        columns = pl.ds(pl.multiple_of(n * HEAD, HEAD), HEAD)
+        piece, partial = b.wide.at[WIDE_CHUNKS, :, :, columns], b.partial.at[2, :, columns]
+        arrived(b, b.wide.at[WIDE_CHUNKS, pl.ds(0, 4)], b.weight_recv.at[WIDE_CHUNKS + n, 3])
+        project_early(b, piece, partial)
+
+        @pl.when(n == 0)
+        def _():
+            pass_second(b, CHUNKS - 1)
+
+        arrived(b, b.wide.at[WIDE_CHUNKS, pl.ds(0, 4)], b.weight_recv.at[WIDE_CHUNKS + n, 4])
+        project_late(b, piece, partial)
+        attend_kept(b, 2 * (WIDE_CHUNKS - 1) + n, (0,))
 
     for j in range(CHUNKS):
         left(b, chunk(b, j).at[pl.ds(0, PIECES - 2)], b.weight_send.at[j])

time: 86.1 us -> 86.3 us (level)
  no operation moved by 1% of the time
where the time goes in v5:
time: 86.3 us; the launch traced here: 86.2 us
  Pallas kernels  86.1 us (100%)
    pallas_call x1, Pallas kernels, body(): pl.pallas_call(kernel, out_shape=pltpu.VMEM(shape, jnp.bfloat16), in_spec...  84.7 us

profile of v5, /device:TPU:1, one launch (start us, length us, event | category | flops | bytes accessed | tf_op | source)
XLA Modules:
  0.0 86.2 jit_solution(3363192469573491715)
XLA Ops:
  0.0 84.7 %packed_attention.1.src = bf16[1,128,8192]{2,1,0:T(8,128)(2,1)S(1)} custom-call(bf16[1,128,5120]{2,1,0:T(8,128)(2,1)} %refs_0_.1, s32[1,1024]{1,0:T(1,128)} %refs_1_.1, s32[1,64]{1,0:T(1,128)} %refs_2_.1, f32[1,5120]{1,0:T(1,128)} %bitcast.9, f32[1,128]{1,0:T(1,128)} %bitcast.10, f32[1,128]{1,0:T(1,128)} %bitcast.11, bf16[2,160,1024]{2,1,0:T(8,128)(2,1)} %bitcast.6, ...), custom_call_target="tpu_custom_call" | custom-call | tf_op jit(solution)/shard_map/packed_attention/pallas_call | solution.py:576
  84.7 1.3 %hand_over.1 = bf16[1,128,8192]{2,1,0:T(8,128)(2,1)} custom-call(bf16[1,128,8192]{2,1,0:T(8,128)(2,1)S(1)} %packed_attention.1.src), custom_call_target="tpu_custom_call" | custom-call | tf_op jit(solution)/shard_map/hand_over/pallas_call | solution.py:597

commit v6 on v4

--- a/solution.py
+++ b/solution.py
@@ -125,14 +125,15 @@
         second_send(b, j, kind)
 
 
+QUEUE = (((1, 1), (2, 0)), ((2, 1), (3, 0)), ((3, 1),), ((4, 0), (4, 1), (5, 0)), ((5, 1),), ())
+
+
 def pass_second(b, j):
     arrived(b, chunk(b, j).at[pl.ds(0, 8)], b.weight_recv.at[j, 2])
     for kind in (2, 5):
         second_send(b, j, kind)
-    if j + 1 < CHUNKS:
-        begin_second(b, j + 1, 1)
-    if j + 2 < CHUNKS:
-        begin_second(b, j + 2, 0)
+    for other, part in QUEUE[j]:
+        begin_second(b, other, part)
 
 
 def finish_second(b, j, part):

time: 86.1 us -> 87.4 us (1.015)
  Pallas kernels: 85.9 us -> 87.1 us
    pallas_call x1, Pallas kernels: 84.5 us -> 85.8 us  [body(): pl.pallas_call(kernel, out_shape=pltpu.VMEM(shape, jnp.bfloat16), in_spec...]
where the time goes in v6:
time: 87.4 us; the launch traced here: 87.3 us
  Pallas kernels  87.1 us (100%)
    pallas_call x1, Pallas kernels, body(): pl.pallas_call(kernel, out_shape=pltpu.VMEM(shape, jnp.bfloat16), in_spec...  85.8 us

profile of v6, /device:TPU:1, one launch (start us, length us, event | category | flops | bytes accessed | tf_op | source)
XLA Modules:
  0.0 87.3 jit_solution(6464327389972611606)
XLA Ops:
  0.0 85.8 %packed_attention.1.src = bf16[1,128,8192]{2,1,0:T(8,128)(2,1)S(1)} custom-call(bf16[1,128,5120]{2,1,0:T(8,128)(2,1)} %refs_0_.1, s32[1,1024]{1,0:T(1,128)} %refs_1_.1, s32[1,64]{1,0:T(1,128)} %refs_2_.1, f32[1,5120]{1,0:T(1,128)} %bitcast.9, f32[1,128]{1,0:T(1,128)} %bitcast.10, f32[1,128]{1,0:T(1,128)} %bitcast.11, bf16[2,160,1024]{2,1,0:T(8,128)(2,1)} %bitcast.6, ...), custom_call_target="tpu_custom_call" | custom-call | tf_op jit(solution)/shard_map/packed_attention/pallas_call | solution.py:570
  85.8 1.3 %hand_over.1 = bf16[1,128,8192]{2,1,0:T(8,128)(2,1)} custom-call(bf16[1,128,8192]{2,1,0:T(8,128)(2,1)S(1)} %packed_attention.1.src), custom_call_target="tpu_custom_call" | custom-call | tf_op jit(solution)/shard_map/hand_over/pallas_call | solution.py:591
